TPU v7x, 256 devices: a whole 4x4x8 slice. The times are simulated.
256 devices in a mesh: gx: 16 (over y, x), gy: 16 (over z, core).
Axes of the slice: x: 4, y: 4, z: 8, core: 2. Of those that a mesh axis runs over, the one named last changes fastest.
Arguments:
- coords: float32 [3, 1048576], P(None, ('gx', 'gy')), may hold values from 0 to 8
- noise: float32 [1048576], P(('gx', 'gy')), may hold values from 0.5 to 2
- order: int32 [16, 65536], P('gx', 'gy'), may hold values from 0 to 65535, as said below
- probes: bfloat16 [64, 1048576], P(None, ('gx', 'gy')), may hold values from -5 to 5
- factors: bfloat16 [10, 2, 32, 1048576], P(None, None, None, ('gx', 'gy')), may hold values from -1 to 1
Outputs:
- product: float32 [64, 1048576], P(None, ('gx', 'gy'))
Inputs may be any that keep to these rules, and one draw needn't show every extreme that they name: Each row of order lists every number from 0 to 65535 once; every run of 4096 tree positions starting at a multiple of 4096 takes exactly 256 numbers from each run of 4096 input indices starting at a multiple of 4096.
All inputs are finite; a program needn't handle non-finite values.
Results may differ from a plain program's by a relative error of at most 0.0029.
Values may be sent and summed in bfloat16 or wider, within the bound.
A program may use at most 128 MiB of HBM per device.

v0:
```python
import jax
import jax.numpy as jnp
from jax import lax
from jax.sharding import PartitionSpec as P

LEAF = 1024


SQRT_THREE = 1.7320508075688772


def swapped(array, axis, stride):
    return lax.ppermute(array, axis, [(i, i ^ 1 << stride) for i in range(lax.axis_size(axis))])


def leaf_kernel(spots, spread):
    square = (spots[0][:, None] - spots[0][None, :]) ** 2
    square = square + (spots[1][:, None] - spots[1][None, :]) ** 2
    square = square + (spots[2][:, None] - spots[2][None, :]) ** 2
    scaled = jnp.sqrt(square) * SQRT_THREE
    return ((1.0 + scaled) * jnp.exp(-scaled) + jnp.diag(spread)).astype(jnp.bfloat16)


def local_term(pair, probes, width):
    total = probes.shape[1]
    nodes = total // width
    rank_size = pair.shape[1]
    count = probes.shape[0]
    right = pair[1].reshape(rank_size, nodes, width)
    left = pair[0].reshape(rank_size, nodes, width)
    vectors = probes.reshape(count, nodes, width)
    coeff = jnp.einsum("rkn,pkn->krp", right, vectors, preferred_element_type=jnp.float32)
    sibling = (
        coeff.reshape(nodes // 2, 2, rank_size, count)[:, ::-1]
        .reshape(nodes, rank_size, count)
        .astype(jnp.bfloat16)
    )
    return jnp.einsum("rkn,krp->pkn", left, sibling, preferred_element_type=jnp.float32).reshape(
        count, total
    )


def pair_inner(values, step_bit):
    return swapped(values, "gy", step_bit)


def sibling_inner(values, step_bit):
    return swapped(values.astype(jnp.bfloat16), "gy", step_bit)


def local(coords, noise, order, probes, factors):
    points = probes.shape[1]
    picks = order[0]
    whole_coords, whole_noise = (
        lax.all_gather(coords, "gy", axis=1, tiled=True),
        lax.all_gather(noise, "gy", axis=0, tiled=True),
    )
    tree_coords = jnp.take(whole_coords, picks, axis=1)
    tree_noise = jnp.take(whole_noise, picks, axis=0)
    blocks = []
    for leaf_index in range(points // LEAF):
        start = leaf_index * LEAF
        kernel = leaf_kernel(tree_coords[:, start : start + LEAF], tree_noise[start : start + LEAF])
        blocks.append(
            jnp.dot(probes[:, start : start + LEAF], kernel, preferred_element_type=jnp.float32)
        )
    product = jnp.concatenate(blocks, axis=1)
    local_levels = (points // LEAF).bit_length() - 1
    for tier_index in range(local_levels):
        product = product + local_term(factors[tier_index], probes, LEAF * 2**tier_index)
    inner_bits = lax.axis_size("gy").bit_length() - 1
    outer_bits = lax.axis_size("gx").bit_length() - 1
    device_levels = inner_bits + outer_bits
    level_terms = [
        jnp.einsum(
            "rn,pn->rp",
            factors[local_levels + height, 1],
            probes,
            preferred_element_type=jnp.float32,
        )
        for height in range(device_levels)
    ]
    siblings = [None] * device_levels
    upper_terms = []
    for height in range(device_levels):
        running = level_terms[height]
        for step_bit in range(min(height, inner_bits)):
            running = running + pair_inner(running, step_bit)
        if height < inner_bits:
            siblings[height] = sibling_inner(running, height)
        else:
            upper_terms.append(running)
    pending = jnp.stack(upper_terms)
    for step_bit in range(outer_bits):
        siblings[inner_bits + step_bit] = swapped(
            pending[step_bit].astype(jnp.bfloat16), "gx", step_bit
        )
        if step_bit + 1 < outer_bits:
            arrived = swapped(pending[step_bit + 1 :], "gx", step_bit)
            pending = jnp.concatenate(
                [pending[: step_bit + 1], pending[step_bit + 1 :] + arrived], axis=0
            )
    for height in range(device_levels):
        product = product + jnp.einsum(
            "rn,rp->pn",
            factors[local_levels + height, 0],
            siblings[height],
            preferred_element_type=jnp.float32,
        )
    return product


def solution(mesh):
    return jax.shard_map(
        local,
        mesh=mesh,
        in_specs=(
            P(None, ("gx", "gy")),
            P(("gx", "gy")),
            P("gx", "gy"),
            P(None, ("gx", "gy")),
            P(None, None, None, ("gx", "gy")),
        ),
        out_specs=P(None, ("gx", "gy")),
        check_vma=False,
    )
```

profile of v0, /device:TPU:16, one launch (start us, length us, event | category | flops | bytes accessed | tf_op | source)
XLA Modules:
  0.0 371.0 jit_solution(6906527651102176689)
XLA Ops:
  0.0 2.0 fusion.32
  4.0 2.0 fusion.28
  7.9 2.0 fusion.48
  11.3 2.1 fusion.92
  14.6 1.8 convolution_convert_fusion
  16.5 20.7 %all_gather.7 = f32[65536]{0:T(1024)S(1)} all-gather(f32[4096]{0:T(1024)S(1)} %copy-done.6), channel_id=1, replica_groups=mesh['gx'=16,'gy'=16] {'gy'}, dimensions={0}, use_global_device_ids=true | all-gather | bytes 278528 | tf_op jit(solution)/shard_map/all_gather | solution.py:56
  37.8 193.2 %all_gather.6 = f32[3,65536]{0,1:T(8,128)} all-gather(f32[3,4096]{0,1:T(8,128)S(1)} %copy.25), channel_id=1, replica_groups=mesh['gx'=16,'gy'=16] {'gy'}, dimensions={1}, use_global_device_ids=true | all-gather | bytes 835584 | tf_op jit(solution)/shard_map/all_gather | solution.py:55
  231.0 23.0 %gather_fusion.1 = f32[4096]{0:T(1024)S(1)} fusion(f32[65536]{0:T(1024)S(1)} %all_gather.7, s32[4096]{0:T(1024)S(1)} %broadcast_clamp_fusion), kind=kCustom, calls=%fused_computation.1 | custom fusion | bytes 49152 | tf_op jit(solution)/shard_map/jit(_take)/gather | solution.py:59
  254.0 21.3 %gather_fusion = f32[4096,3]{1,0:T(8,128)S(1)} fusion(f32[3,65536]{0,1:T(8,128)} %all_gather.6, s32[4096]{0:T(1024)S(1)} %broadcast_clamp_fusion), kind=kCustom, calls=%fused_computation | custom fusion | bytes 114688 | tf_op jit(solution)/shard_map/jit(_take)/gather | solution.py:58
  275.4 2.3 select_bitcast_fusion
  277.7 2.8 slice_reduce_fusion.11
  281.7 3.3 fusion.14
  284.9 3.3 fusion.13
  288.2 3.5 fusion.12
  291.7 3.3 fusion.11
  309.7 2.8 collective-permute-start.21
  312.8 3.0 collective-permute-start.12
  316.2 4.7 %collective-permute-done.8 = f32[32,64]{1,0:T(8,128)S(1)} collective-permute-done((f32[32,64]{1,0:T(8,128)S(1)}, f32[32,64]{1,0:T(8,128)S(1)}, u32[]{:S(2)}, u32[]{:S(2)}) %collective-permute-start.8) | collective-permute-done | bytes 8224 | tf_op jit(solution)/shard_map/ppermute | solution.py:13
  320.8 4.6 %collective-permute-done.5 = bf16[32,64]{1,0:T(8,128)(2,1)S(1)} collective-permute-done((bf16[32,64]{1,0:T(8,128)(2,1)S(1)}, bf16[32,64]{1,0:T(8,128)(2,1)S(1)}, u32[]{:S(2)}, u32[]{:S(2)}) %collective-permute-start.5) | collective-permute-done | bytes 4128 | tf_op jit(solution)/shard_map/ppermute | solution.py:13
  325.5 2.0 collective-permute-start.9
  328.9 4.0 %collective-permute-start.18 = (f32[32,64]{1,0:T(8,128)S(1)}, f32[32,64]{1,0:T(8,128)S(1)}, u32[]{:S(2)}, u32[]{:S(2)}) collective-permute-start(f32[32,64]{1,0:T(8,128)S(1)} %add.217), channel_id=1, source_target_pairs={{0,8},{1,9},{2,10},{3,11},{4,12},{5,13},{6,14},{7,15},{8,0},{9,1},... | collective-permute-start | bytes 24584 | tf_op jit(solution)/shard_map/ppermute | solution.py:13
  332.9 2.1 collective-permute-start.22
  335.0 4.0 %collective-permute-start.26 = (f32[32,64]{1,0:T(8,128)S(1)}, f32[32,64]{1,0:T(8,128)S(1)}, u32[]{:S(2)}, u32[]{:S(2)}) collective-permute-start(f32[32,64]{1,0:T(8,128)S(1)} %add.225), channel_id=1, source_target_pairs={{0,8},{1,9},{2,10},{3,11},{4,12},{5,13},{6,14},{7,15},{8,0},{9,1},... | collective-permute-start | bytes 24584 | tf_op jit(solution)/shard_map/ppermute | solution.py:13
  339.0 2.1 collective-permute-start.13
  342.8 1.5 collective-permute-start.27
  344.3 2.4 collective-permute-done.13
  348.0 2.8 collective-permute-start.28
  352.1 2.7 collective-permute-start.29
  356.1 1.6 collective-permute-done.29
  359.7 1.7 collective-permute-done.31
  363.9 2.7 collective-permute-done.32
  367.9 2.7 fusion.6
  (124 shorter events, 36.3 us)
Async XLA Ops:
  2.1 294.7 %collective-permute-start.15 = (f32[32,64]{1,0:T(8,128)}, f32[32,64]{1,0:T(8,128)}, u32[]{:S(2)}, u32[]{:S(2)}) collective-permute-start(f32[32,64]{1,0:T(8,128)} %fusion.32), channel_id=1, source_target_pairs={{0,1},{1,0},{2,3},{3,2},{4,5},{5,4},{6,7},{7,6},{8,9},{9,8},{10,11... | collective-permute-start | bytes 24584 | tf_op jit(solution)/shard_map/ppermute | solution.py:13
  3.5 294.2 %collective-permute-start.19 = (f32[32,64]{1,0:T(8,128)S(1)}, f32[32,64]{1,0:T(8,128)}, u32[]{:S(2)}, u32[]{:S(2)}) collective-permute-start(f32[32,64]{1,0:T(8,128)S(1)} %fusion.30), channel_id=1, source_target_pairs={{0,1},{1,0},{2,3},{3,2},{4,5},{5,4},{6,7},{7,6},{8,9},{9,8},{10,11... | collective-permute-start | bytes 24584 | tf_op jit(solution)/shard_map/ppermute | solution.py:13
  6.0 293.0 %collective-permute-start.23 = (f32[32,64]{1,0:T(8,128)}, f32[32,64]{1,0:T(8,128)}, u32[]{:S(2)}, u32[]{:S(2)}) collective-permute-start(f32[32,64]{1,0:T(8,128)} %fusion.28), channel_id=1, source_target_pairs={{0,1},{1,0},{2,3},{3,2},{4,5},{5,4},{6,7},{7,6},{8,9},{9,8},{10,11... | collective-permute-start | bytes 24584 | tf_op jit(solution)/shard_map/ppermute | solution.py:13
  7.4 294.4 %collective-permute-start.10 = (f32[32,64]{1,0:T(8,128)S(1)}, f32[32,64]{1,0:T(8,128)}, u32[]{:S(2)}, u32[]{:S(2)}) collective-permute-start(f32[32,64]{1,0:T(8,128)S(1)} %fusion.36), channel_id=1, source_target_pairs={{0,1},{1,0},{2,3},{3,2},{4,5},{5,4},{6,7},{7,6},{8,9},{9,8},{10,11... | collective-permute-start | bytes 24584 | tf_op jit(solution)/shard_map/ppermute | solution.py:13
  9.9 285.6 %collective-permute-start.1 = (f32[32,64]{1,0:T(8,128)}, f32[32,64]{1,0:T(8,128)}, u32[]{:S(2)}, u32[]{:S(2)}) collective-permute-start(f32[32,64]{1,0:T(8,128)} %fusion.48), channel_id=1, source_target_pairs={{0,1},{1,0},{2,3},{3,2},{4,5},{5,4},{6,7},{7,6},{8,9},{9,8},{10,11... | collective-permute-start | bytes 24584 | tf_op jit(solution)/shard_map/ppermute | solution.py:13
  295.5 8.3 %collective-permute-start.6 = (f32[32,64]{1,0:T(8,128)S(1)}, f32[32,64]{1,0:T(8,128)S(1)}, u32[]{:S(2)}, u32[]{:S(2)}) collective-permute-start(f32[32,64]{1,0:T(8,128)S(1)} %fusion.40), channel_id=1, source_target_pairs={{0,1},{1,0},{2,3},{3,2},{4,5},{5,4},{6,7},{7,6},{8,9},{9,8},{10,11... | collective-permute-start | bytes 24584 | tf_op jit(solution)/shard_map/ppermute | solution.py:13
  296.7 7.9 %collective-permute-start.3 = (f32[32,64]{1,0:T(8,128)S(1)}, f32[32,64]{1,0:T(8,128)S(1)}, u32[]{:S(2)}, u32[]{:S(2)}) collective-permute-start(f32[32,64]{1,0:T(8,128)S(1)} %fusion.44), channel_id=1, source_target_pairs={{0,1},{1,0},{2,3},{3,2},{4,5},{5,4},{6,7},{7,6},{8,9},{9,8},{10,11... | collective-permute-start | bytes 24584 | tf_op jit(solution)/shard_map/ppermute | solution.py:13
  297.7 9.2 %collective-permute-start.16 = (f32[32,64]{1,0:T(8,128)S(1)}, f32[32,64]{1,0:T(8,128)S(1)}, u32[]{:S(2)}, u32[]{:S(2)}) collective-permute-start(f32[32,64]{1,0:T(8,128)S(1)} %add.215), channel_id=1, source_target_pairs={{0,2},{1,3},{2,0},{3,1},{4,6},{5,7},{6,4},{7,5},{8,10},{9,11},{10,... | collective-permute-start | bytes 24584 | tf_op jit(solution)/shard_map/ppermute | solution.py:13
  299.0 7.0 %collective-permute-start.2 = (bf16[32,64]{1,0:T(8,128)(2,1)S(1)}, bf16[32,64]{1,0:T(8,128)(2,1)S(1)}, u32[]{:S(2)}, u32[]{:S(2)}) collective-permute-start(bf16[32,64]{1,0:T(8,128)(2,1)S(1)} %add_convert_fusion.20), channel_id=1, source_target_pairs={{0,2},{1,3},{2,0},{3,1},{4,6},{5,7},{6,4},{7,5},{8,10},{9,11},{10,... | collective-permute-start | bytes 12296 | tf_op jit(solution)/shard_map/ppermute | solution.py:13
  301.8 7.5 %collective-permute-start.20 = (f32[32,64]{1,0:T(8,128)S(1)}, f32[32,64]{1,0:T(8,128)S(1)}, u32[]{:S(2)}, u32[]{:S(2)}) collective-permute-start(f32[32,64]{1,0:T(8,128)S(1)} %add.219), channel_id=1, source_target_pairs={{0,2},{1,3},{2,0},{3,1},{4,6},{5,7},{6,4},{7,5},{8,10},{9,11},{10,... | collective-permute-start | bytes 24584 | tf_op jit(solution)/shard_map/ppermute | solution.py:13
  303.8 5.9 %collective-permute-start.24 = (f32[32,64]{1,0:T(8,128)S(1)}, f32[32,64]{1,0:T(8,128)S(1)}, u32[]{:S(2)}, u32[]{:S(2)}) collective-permute-start(f32[32,64]{1,0:T(8,128)S(1)} %add.223), channel_id=1, source_target_pairs={{0,2},{1,3},{2,0},{3,1},{4,6},{5,7},{6,4},{7,5},{8,10},{9,11},{10,... | collective-permute-start | bytes 24584 | tf_op jit(solution)/shard_map/ppermute | solution.py:13
  304.7 7.8 %collective-permute-start.11 = (f32[32,64]{1,0:T(8,128)S(1)}, f32[32,64]{1,0:T(8,128)S(1)}, u32[]{:S(2)}, u32[]{:S(2)}) collective-permute-start(f32[32,64]{1,0:T(8,128)S(1)} %add.210), channel_id=1, source_target_pairs={{0,2},{1,3},{2,0},{3,1},{4,6},{5,7},{6,4},{7,5},{8,10},{9,11},{10,... | collective-permute-start | bytes 24584 | tf_op jit(solution)/shard_map/ppermute | solution.py:13
  306.0 6.8 %collective-permute-start.7 = (f32[32,64]{1,0:T(8,128)S(1)}, f32[32,64]{1,0:T(8,128)S(1)}, u32[]{:S(2)}, u32[]{:S(2)}) collective-permute-start(f32[32,64]{1,0:T(8,128)S(1)} %add.206), channel_id=1, source_target_pairs={{0,2},{1,3},{2,0},{3,1},{4,6},{5,7},{6,4},{7,5},{8,10},{9,11},{10,... | collective-permute-start | bytes 24584 | tf_op jit(solution)/shard_map/ppermute | solution.py:13
  306.9 9.0 %collective-permute-start.4 = (f32[32,64]{1,0:T(8,128)S(1)}, f32[32,64]{1,0:T(8,128)S(1)}, u32[]{:S(2)}, u32[]{:S(2)}) collective-permute-start(f32[32,64]{1,0:T(8,128)S(1)} %add.203), channel_id=1, source_target_pairs={{0,2},{1,3},{2,0},{3,1},{4,6},{5,7},{6,4},{7,5},{8,10},{9,11},{10,... | collective-permute-start | bytes 24584 | tf_op jit(solution)/shard_map/ppermute | solution.py:13
  309.4 19.4 %collective-permute-start.17 = (f32[32,64]{1,0:T(8,128)S(1)}, f32[32,64]{1,0:T(8,128)S(1)}, u32[]{:S(2)}, u32[]{:S(2)}) collective-permute-start(f32[32,64]{1,0:T(8,128)S(1)} %add.216), channel_id=1, source_target_pairs={{0,4},{1,5},{2,6},{3,7},{4,0},{5,1},{6,2},{7,3},{8,12},{9,13},{10,... | collective-permute-start | bytes 24584 | tf_op jit(solution)/shard_map/ppermute | solution.py:13
  309.7 19.2 %collective-permute-start.21 = (f32[32,64]{1,0:T(8,128)S(1)}, f32[32,64]{1,0:T(8,128)S(1)}, u32[]{:S(2)}, u32[]{:S(2)}) collective-permute-start(f32[32,64]{1,0:T(8,128)S(1)} %add.220), channel_id=1, source_target_pairs={{0,4},{1,5},{2,6},{3,7},{4,0},{5,1},{6,2},{7,3},{8,12},{9,13},{10,... | collective-permute-start | bytes 24584 | tf_op jit(solution)/shard_map/ppermute | solution.py:13
  312.5 20.4 %collective-permute-start.25 = (f32[32,64]{1,0:T(8,128)S(1)}, f32[32,64]{1,0:T(8,128)S(1)}, u32[]{:S(2)}, u32[]{:S(2)}) collective-permute-start(f32[32,64]{1,0:T(8,128)S(1)} %add.224), channel_id=1, source_target_pairs={{0,4},{1,5},{2,6},{3,7},{4,0},{5,1},{6,2},{7,3},{8,12},{9,13},{10,... | collective-permute-start | bytes 24584 | tf_op jit(solution)/shard_map/ppermute | solution.py:13
  312.8 22.2 %collective-permute-start.12 = (f32[32,64]{1,0:T(8,128)S(1)}, f32[32,64]{1,0:T(8,128)S(1)}, u32[]{:S(2)}, u32[]{:S(2)}) collective-permute-start(f32[32,64]{1,0:T(8,128)S(1)} %add.211), channel_id=1, source_target_pairs={{0,4},{1,5},{2,6},{3,7},{4,0},{5,1},{6,2},{7,3},{8,12},{9,13},{10,... | collective-permute-start | bytes 24584 | tf_op jit(solution)/shard_map/ppermute | solution.py:13
  315.8 5.0 %collective-permute-start.8 = (f32[32,64]{1,0:T(8,128)S(1)}, f32[32,64]{1,0:T(8,128)S(1)}, u32[]{:S(2)}, u32[]{:S(2)}) collective-permute-start(f32[32,64]{1,0:T(8,128)S(1)} %add.207), channel_id=1, source_target_pairs={{0,4},{1,5},{2,6},{3,7},{4,0},{5,1},{6,2},{7,3},{8,12},{9,13},{10,... | collective-permute-start | bytes 24584 | tf_op jit(solution)/shard_map/ppermute | solution.py:13
  320.8 4.6 %collective-permute-start.5 = (bf16[32,64]{1,0:T(8,128)(2,1)S(1)}, bf16[32,64]{1,0:T(8,128)(2,1)S(1)}, u32[]{:S(2)}, u32[]{:S(2)}) collective-permute-start(bf16[32,64]{1,0:T(8,128)(2,1)S(1)} %add_convert_fusion.19), channel_id=1, source_target_pairs={{0,4},{1,5},{2,6},{3,7},{4,0},{5,1},{6,2},{7,3},{8,12},{9,13},{10,... | collective-permute-start | bytes 12296 | tf_op jit(solution)/shard_map/ppermute | solution.py:13
  325.5 13.6 %collective-permute-start.9 = (bf16[32,64]{1,0:T(8,128)(2,1)S(1)}, bf16[32,64]{1,0:T(8,128)(2,1)S(1)}, u32[]{:S(2)}, u32[]{:S(2)}) collective-permute-start(bf16[32,64]{1,0:T(8,128)(2,1)S(1)} %add_convert_fusion.18), channel_id=1, source_target_pairs={{0,8},{1,9},{2,10},{3,11},{4,12},{5,13},{6,14},{7,15},{8,0},{9,1},... | collective-permute-start | bytes 12296 | tf_op jit(solution)/shard_map/ppermute | solution.py:13
  328.8 39.1 %collective-permute-start = (bf16[32,64]{1,0:T(8,128)(2,1)S(1)}, bf16[32,64]{1,0:T(8,128)(2,1)S(1)}, u32[]{:S(2)}, u32[]{:S(2)}) collective-permute-start(bf16[32,64]{1,0:T(8,128)(2,1)S(1)} %copy-done.7), channel_id=1, source_target_pairs={{0,1},{1,0},{2,3},{3,2},{4,5},{5,4},{6,7},{7,6},{8,9},{9,8},{10,11... | collective-permute-start | bytes 12296 | tf_op jit(solution)/shard_map/ppermute | solution.py:13
  328.9 13.5 %collective-permute-start.18 = (f32[32,64]{1,0:T(8,128)S(1)}, f32[32,64]{1,0:T(8,128)S(1)}, u32[]{:S(2)}, u32[]{:S(2)}) collective-permute-start(f32[32,64]{1,0:T(8,128)S(1)} %add.217), channel_id=1, source_target_pairs={{0,8},{1,9},{2,10},{3,11},{4,12},{5,13},{6,14},{7,15},{8,0},{9,1},... | collective-permute-start | bytes 24584 | tf_op jit(solution)/shard_map/ppermute | solution.py:13
  332.9 9.5 %collective-permute-start.22 = (f32[32,64]{1,0:T(8,128)S(1)}, f32[32,64]{1,0:T(8,128)S(1)}, u32[]{:S(2)}, u32[]{:S(2)}) collective-permute-start(f32[32,64]{1,0:T(8,128)S(1)} %add.221), channel_id=1, source_target_pairs={{0,8},{1,9},{2,10},{3,11},{4,12},{5,13},{6,14},{7,15},{8,0},{9,1},... | collective-permute-start | bytes 24584 | tf_op jit(solution)/shard_map/ppermute | solution.py:13
  335.0 7.8 %collective-permute-start.26 = (f32[32,64]{1,0:T(8,128)S(1)}, f32[32,64]{1,0:T(8,128)S(1)}, u32[]{:S(2)}, u32[]{:S(2)}) collective-permute-start(f32[32,64]{1,0:T(8,128)S(1)} %add.225), channel_id=1, source_target_pairs={{0,8},{1,9},{2,10},{3,11},{4,12},{5,13},{6,14},{7,15},{8,0},{9,1},... | collective-permute-start | bytes 24584 | tf_op jit(solution)/shard_map/ppermute | solution.py:13
  339.0 7.7 %collective-permute-start.13 = (f32[32,64]{1,0:T(8,128)S(1)}, f32[32,64]{1,0:T(8,128)S(1)}, u32[]{:S(2)}, u32[]{:S(2)}) collective-permute-start(f32[32,64]{1,0:T(8,128)S(1)} %add.212), channel_id=1, source_target_pairs={{0,8},{1,9},{2,10},{3,11},{4,12},{5,13},{6,14},{7,15},{8,0},{9,1},... | collective-permute-start | bytes 24584 | tf_op jit(solution)/shard_map/ppermute | solution.py:13
  342.8 5.2 %collective-permute-start.27 = (f32[3,32,64]{2,1,0:T(8,128)S(1)}, f32[3,32,64]{2,1,0:T(8,128)S(1)}, u32[]{:S(2)}, u32[]{:S(2)}) collective-permute-start(f32[3,32,64]{2,1,0:T(8,128)S(1)} %pad_maximum_fusion), channel_id=1, source_target_pairs={{0,16},{16,0},{32,48},{48,32},{64,80},{80,64},{96,112},{112,96},{1... | collective-permute-start | bytes 73736 | tf_op jit(solution)/shard_map/ppermute | solution.py:13
  346.7 4.1 %collective-permute-start.14 = (bf16[32,64]{1,0:T(8,128)(2,1)S(1)}, bf16[32,64]{1,0:T(8,128)(2,1)S(1)}, u32[]{:S(2)}, u32[]{:S(2)}) collective-permute-start(bf16[32,64]{1,0:T(8,128)(2,1)S(1)} %add_convert_fusion.17), channel_id=1, source_target_pairs={{0,16},{16,0},{32,48},{48,32},{64,80},{80,64},{96,112},{112,96},{1... | collective-permute-start | bytes 12296 | tf_op jit(solution)/shard_map/ppermute | solution.py:13
  348.0 6.8 %collective-permute-start.28 = (bf16[32,64]{1,0:T(8,128)(2,1)S(1)}, bf16[32,64]{1,0:T(8,128)(2,1)S(1)}, u32[]{:S(2)}, u32[]{:S(2)}) collective-permute-start(bf16[32,64]{1,0:T(8,128)(2,1)S(1)} %fusion.77), channel_id=1, source_target_pairs={{0,32},{16,48},{32,0},{48,16},{64,96},{80,112},{96,64},{112,80},{1... | collective-permute-start | bytes 12296 | tf_op jit(solution)/shard_map/ppermute | solution.py:13
  352.1 5.5 %collective-permute-start.29 = (f32[2,32,64]{2,1,0:T(8,128)S(1)}, f32[2,32,64]{2,1,0:T(8,128)S(1)}, u32[]{:S(2)}, u32[]{:S(2)}) collective-permute-start(f32[2,32,64]{2,1,0:T(8,128)S(1)} %slice.242), channel_id=1, source_target_pairs={{0,32},{16,48},{32,0},{48,16},{64,96},{80,112},{96,64},{112,80},{1... | collective-permute-start | bytes 49160 | tf_op jit(solution)/shard_map/ppermute | solution.py:13
  357.6 3.8 %collective-permute-start.31 = (f32[1,32,64]{2,1,0:T(8,128)S(1)}, f32[1,32,64]{2,1,0:T(8,128)S(1)}, u32[]{:S(2)}, u32[]{:S(2)}) collective-permute-start(f32[1,32,64]{2,1,0:T(8,128)S(1)} %slice.244), channel_id=1, source_target_pairs={{0,64},{16,80},{32,96},{48,112},{64,0},{80,16},{96,32},{112,48},{1... | collective-permute-start | bytes 24584 | tf_op jit(solution)/shard_map/ppermute | solution.py:13
  361.5 5.2 %collective-permute-start.32 = (bf16[32,64]{1,0:T(8,128)(2,1)S(1)}, bf16[32,64]{1,0:T(8,128)(2,1)S(1)}, u32[]{:S(2)}, u32[]{:S(2)}) collective-permute-start(bf16[32,64]{1,0:T(8,128)(2,1)S(1)} %fusion.76), channel_id=1, source_target_pairs={{0,128},{16,144},{32,160},{48,176},{64,192},{80,208},{96,224},{112... | collective-permute-start | bytes 12296 | tf_op jit(solution)/shard_map/ppermute | solution.py:13
  (9 other events, 166.7 us)
where the time goes:
time: 377 us; the launch traced here: 371 us
  blocking collectives  214 us (57%)
  local copies, waits for them, and re-layouts  50.8 us (13%)
  starting transfers between devices  41.2 us (11%)
  matrix products  39.3 us (10%)
  waiting for transfers between devices  18.9 us (5%)
  other arithmetic  6.12 us (2%)
    all_gather x1, blocking collectives, local(): lax.all_gather(coords, 'gy', axis=1, tiled=True)  193 us
    ppermute x33, starting transfers between devices, swapped(): lax.ppermute(array, axis, [(i, i ^ 1 << stride) for i in range(lax.axis_s...  41.2 us
    gather x1, local copies, waits for them, and re-layouts, local(): tree_noise = jnp.take(whole_noise, picks, axis=0)  23 us
    gather x1, local copies, waits for them, and re-layouts, local(): tree_coords = jnp.take(whole_coords, picks, axis=1)  21.3 us
    all_gather x1, blocking collectives, local(): lax.all_gather(noise, 'gy', axis=0, tiled=True)  20.7 us
    ppermute x33, waiting for transfers between devices, swapped(): lax.ppermute(array, axis, [(i, i ^ 1 << stride) for i in range(lax.axis_s...  18.9 us
    dot_general x4, matrix products, local(): jnp.dot(probes[:, start:start + LEAF], kernel, preferred_element_type=jnp...  13.3 us
    dot_general x8, matrix products, local(): jnp.einsum('rn,pn->rp', factors[local_levels + height, 1], probes, prefer...  13.2 us
  transfers between devices with their start and end apart: 33, of which 8 were waited for; matrix products, arithmetic and copies ran while one was open for 25% of the time, Pallas kernels for 0%

commit v1 on v0

v1 whole, which is shorter than its diff:
```python
import functools

import jax
import jax.numpy as jnp
from jax import lax
from jax.experimental import pallas as pl
from jax.experimental.pallas import tpu as pltpu
from jax.sharding import PartitionSpec as P

LEAF = 1024
RANK = 32
PROBES = 64
LANES = 128
TILE = 256
NT = (((1,), (1,)), ((), ()))
TN = (((0,), (0,)), ((), ()))
SQRT_THREE = 1.7320508075688772


def dot(a, b, dims=(((1,), (0,)), ((), ()))):
    return lax.dot_general(a, b, dims, preferred_element_type=jnp.float32)


def look_up(table, first, second):
    shape = (8, LANES)
    found = []
    for picks in (first, second):
        picks = jnp.broadcast_to(picks, shape)
        lane = picks & (LANES - 1)
        upper = picks >> 8
        out = jnp.zeros(shape, jnp.float32)
        for r, vector in enumerate(table):
            out = jnp.where(
                upper == r,
                jnp.take_along_axis(vector, lane, axis=1, mode="promise_in_bounds"),
                out,
            )
        found.append((out, ((picks >> 7) & 1) == 0))
    row = lax.broadcasted_iota(jnp.int32, shape, 0)
    (one, one_low), (two, two_low) = found
    return jnp.where(
        row < 4,
        jnp.where(one_low, one, pltpu.roll(one, 4, 0)),
        jnp.where(two_low, pltpu.roll(two, 4, 0), two),
    )


def exchange_kernel(
    inner,
    outer,
    coords_hbm,
    noise_hbm,
    order_hbm,
    probes_hbm,
    factors_hbm,
    tree_ref,
    sib_ref,
    near_ref,
    coords,
    noise,
    order,
    probes,
    right,
    counts,
    slots,
    table,
    ask,
    asked,
    give,
    given,
    part,
    parts,
    inner_sib,
    total,
    totals,
    pairs,
    back,
    backs,
    load_sem,
    send_sem,
    recv_sem,
):
    gx, gy = lax.axis_index("gx"), lax.axis_index("gy")
    points = order.shape[1]
    slot = points // inner
    levels = right.shape[0]
    far = levels - 2
    inner_bits = inner.bit_length() - 1
    outer_bits = outer.bit_length() - 1
    share = PROBES // inner

    barrier = pltpu.get_barrier_semaphore()
    for axis, own, size in (("gy", gy, inner), ("gx", gx, outer)):

        @pl.loop(1, size)
        def _(j):
            pl.semaphore_signal(barrier, inc=1, device_id={axis: lax.rem(own + j, size)})

    loads = [
        pltpu.make_async_copy(source, target, load_sem.at[i])
        for i, (source, target) in enumerate(
            (
                (order_hbm, order),
                (coords_hbm, coords),
                (noise_hbm, noise),
                (probes_hbm, probes),
                (factors_hbm.at[:, 1], right),
            )
        )
    ]
    for load in loads:
        load.start()

    def send(step, source, target, axis, peer):
        pltpu.make_async_remote_copy(
            src_ref=source,
            dst_ref=target,
            send_sem=send_sem.at[step],
            recv_sem=recv_sem.at[step],
            device_id={axis: peer},
        ).start()

    def wait_all(sems, step, ref, count):
        whole = ref.at[pl.ds(0, count)]
        pltpu.make_async_copy(whole, whole, sems.at[step]).wait()

    loads[0].wait()
    wanted = order[...]
    source = ((wanted >> (points.bit_length() - 1)) - gy) & (inner - 1)
    local_index = wanted & (points - 1)
    kind = lax.broadcasted_iota(jnp.int32, (inner, TILE), 0)
    chunks = points // TILE
    for k in range(chunks):
        counts[k * inner : (k + 1) * inner, :] = (
            kind == source[:, k * TILE : (k + 1) * TILE]
        ).astype(jnp.bfloat16)
    before = lax.broadcasted_iota(jnp.int32, (TILE, 2 * TILE), 0)
    column = lax.broadcasted_iota(jnp.int32, (TILE, 2 * TILE), 1)
    ones = ((before < column) | (column >= TILE)).astype(jnp.bfloat16)
    ahead = dot(counts[...], ones)
    offset = jnp.zeros((inner, TILE), jnp.float32)
    for k in range(chunks):
        rows = ahead[k * inner : (k + 1) * inner]
        own_source = source[:, k * TILE : (k + 1) * TILE]
        place = jnp.sum(
            jnp.where(kind == own_source, rows[:, :TILE] + offset, 0.0), axis=0, keepdims=True
        )
        slots[:, k * TILE : (k + 1) * TILE] = own_source * slot + place.astype(jnp.int32)
        offset = offset + rows[:, TILE:]

    place = slots[...]
    upper = lax.broadcasted_iota(jnp.int32, (points // LANES, points), 0) == (place >> 7)
    lower = lax.broadcasted_iota(jnp.int32, (LANES, points), 0) == (place & (LANES - 1))
    low_part = (local_index & 63).astype(jnp.float32)
    high_part = (local_index >> 6).astype(jnp.float32)
    marked = jnp.concatenate(
        [jnp.where(upper, low_part, 0.0), jnp.where(upper, high_part, 0.0)], axis=0
    ).astype(jnp.bfloat16)
    lists = dot(marked, lower.astype(jnp.bfloat16), NT)
    lists = (lists[: points // LANES] + 64.0 * lists[points // LANES :]).astype(jnp.int32)
    for j in range(inner):
        ask[j] = lists[2 * j : 2 * j + 2]

    pl.semaphore_wait(barrier, inner + outer - 2)

    @pl.loop(1, inner)
    def _(j):
        send(0, ask.at[j], asked.at[j - 1], "gy", lax.rem(gy + j, inner))

    loads[3].wait()
    loads[4].wait()
    vectors = probes[...]
    coeff = dot(vectors, right[2:].reshape(far * RANK, points), NT)
    for k in range(inner):
        part[k] = coeff[k * share : (k + 1) * share]
    parts[pl.ds(gy, 1)] = part[pl.ds(gy, 1)]

    @pl.loop(1, inner)
    def _(j):
        peer = lax.rem(gy + j, inner)
        send(2, part.at[peer], parts.at[gy], "gy", peer)

    loads[1].wait()
    loads[2].wait()
    values = jnp.concatenate([coords[...], noise[...]], axis=0)
    vectors_own = [
        jnp.concatenate(
            [values[:, c * LANES : (c + 1) * LANES] for c in (2 * r, 2 * r + 1)], axis=0
        )
        for r in range(points // TILE)
    ]
    for r in range(points // TILE):
        table[r] = vectors_own[r]

    near = [
        dot(
            vectors[:, a * LEAF : (a + 1) * LEAF],
            right[:2, :, a * LEAF : (a + 1) * LEAF].reshape(2 * RANK, LEAF),
            NT,
        )
        for a in range(points // LEAF)
    ]
    level = lax.broadcasted_iota(jnp.int32, (PROBES, 2 * RANK), 1) < RANK
    for a in range(points // LEAF):
        other = 2 * (1 - a // 2)
        near_ref[a] = jnp.where(level, near[a ^ 1], near[other] + near[other + 1]).astype(
            jnp.bfloat16
        )

    own_table = [table[r] for r in range(points // TILE)]
    given[0] = look_up(own_table, ask[0, 0:1], ask[0, 1:2])
    wait_all(recv_sem, 0, asked, inner - 1)

    @pl.loop(1, inner)
    def _(j):
        own_table = [table[r] for r in range(points // TILE)]
        lists = asked[j - 1]
        give[j - 1] = look_up(own_table, lists[0:1], lists[1:2])
        send(1, give.at[j - 1], given.at[j], "gy", lax.rem(gy - j + inner, inner))

    wait_all(recv_sem, 2, parts, inner - 1)
    half = inner_bits * RANK
    lane = lax.broadcasted_iota(jnp.int32, (share, half), 1)
    sums = [[parts[e] for e in range(inner)]]
    for step in range(inner_bits):
        last = sums[-1]
        sums.append([last[2 * g] + last[2 * g + 1] for g in range(len(last) // 2)])
    total[...] = sums[inner_bits][0][:, half:]
    totals[pl.ds(gx, 1)] = total[...][None]

    @pl.loop(1, outer)
    def _(j):
        send(3, total, totals.at[gx], "gx", lax.rem(gx + j, outer))

    for d in range(inner):
        picked = sums[inner_bits - 1][(d >> (inner_bits - 1)) ^ 1][:, :half]
        for h in reversed(range(inner_bits - 1)):
            picked = jnp.where(lane < (h + 1) * RANK, sums[h][(d >> h) ^ 1][:, :half], picked)
        inner_sib[d] = picked

    wait_all(recv_sem, 1, given, inner - 1)
    received = [given[r] for r in range(inner)]
    for k in range(chunks):
        found = look_up(
            received,
            slots[:, 2 * k * LANES : (2 * k + 1) * LANES],
            slots[:, (2 * k + 1) * LANES : (2 * k + 2) * LANES],
        )
        tree_ref[:, 2 * k * LANES : (2 * k + 1) * LANES] = found[0:4]
        tree_ref[:, (2 * k + 1) * LANES : (2 * k + 2) * LANES] = found[4:8]

    wait_all(recv_sem, 3, totals, outer - 1)
    width = outer_bits * RANK
    lane = lax.broadcasted_iota(jnp.int32, (share, width), 1)
    base = 0
    sums = [totals[e] for e in range(outer)]
    picked = None
    for h in range(outer_bits):
        for g, value in enumerate(sums):
            pairs[base + g] = value
        group = gx // 2**h
        sibling = pairs[base + group + 1 - 2 * (group % 2)]
        picked = sibling if picked is None else jnp.where(lane < h * RANK, picked, sibling)
        base += len(sums)
        sums = [sums[2 * g] + sums[2 * g + 1] for g in range(len(sums) // 2)]
    for d in range(inner):
        back[d] = jnp.concatenate([inner_sib[d], picked], axis=1)
    backs[pl.ds(gy, 1)] = back[pl.ds(gy, 1)]

    @pl.loop(1, inner)
    def _(j):
        peer = lax.rem(gy + j, inner)
        send(4, back.at[peer], backs.at[gy], "gy", peer)

    wait_all(recv_sem, 4, backs, inner - 1)
    sib_ref[...] = jnp.concatenate([backs[k] for k in range(inner)], axis=0).astype(jnp.bfloat16)

    wait_all(send_sem, 0, asked, inner - 1)
    wait_all(send_sem, 1, give, inner - 1)
    wait_all(send_sem, 2, part, inner - 1)
    wait_all(send_sem, 3, totals, outer - 1)
    wait_all(send_sem, 4, back, inner - 1)


def exchange(inner, outer, coords, noise, order, probes, factors):
    points = probes.shape[1]
    levels = factors.shape[0]
    far = levels - 2
    share = PROBES // inner
    inner_bits = inner.bit_length() - 1
    outer_bits = outer.bit_length() - 1
    wide = far * RANK
    f32, bf16, i32 = jnp.float32, jnp.bfloat16, jnp.int32
    hbm = pl.BlockSpec(memory_space=pl.ANY)
    vmem = pl.BlockSpec(memory_space=pltpu.VMEM)
    return pl.pallas_call(
        functools.partial(exchange_kernel, inner, outer),
        out_shape=(
            jax.ShapeDtypeStruct((4, points), f32),
            jax.ShapeDtypeStruct((PROBES, wide), bf16),
            jax.ShapeDtypeStruct((points // LEAF, PROBES, 2 * RANK), bf16),
        ),
        in_specs=[hbm] * 5,
        out_specs=(vmem, vmem, vmem),
        scratch_shapes=[
            pltpu.VMEM((3, points), f32),
            pltpu.VMEM((1, points), f32),
            pltpu.VMEM((1, points), i32),
            pltpu.VMEM((PROBES, points), bf16),
            pltpu.VMEM((levels, RANK, points), bf16),
            pltpu.VMEM((inner * points // TILE, TILE), bf16),
            pltpu.VMEM((1, points), i32),
            pltpu.VMEM((points // TILE, 8, LANES), f32),
            pltpu.VMEM((inner, 2, LANES), i32),
            pltpu.VMEM((inner - 1, 2, LANES), i32),
            pltpu.VMEM((inner - 1, 8, LANES), f32),
            pltpu.VMEM((inner, 8, LANES), f32),
            pltpu.VMEM((inner, share, wide), f32),
            pltpu.VMEM((inner, share, wide), f32),
            pltpu.VMEM((inner, share, inner_bits * RANK), f32),
            pltpu.VMEM((share, outer_bits * RANK), f32),
            pltpu.VMEM((outer, share, outer_bits * RANK), f32),
            pltpu.VMEM((2 * outer, share, outer_bits * RANK), f32),
            pltpu.VMEM((inner, share, wide), f32),
            pltpu.VMEM((inner, share, wide), f32),
            pltpu.SemaphoreType.DMA((5,)),
            pltpu.SemaphoreType.DMA((5,)),
            pltpu.SemaphoreType.DMA((5,)),
        ],
        compiler_params=pltpu.CompilerParams(
            collective_id=0, has_side_effects=True, vmem_limit_bytes=40 * 2**20
        ),
    )(coords, noise.reshape(1, points), order, probes, factors)


def split_three(x):
    one = x.astype(jnp.bfloat16)
    rest = x - one.astype(jnp.float32)
    two = rest.astype(jnp.bfloat16)
    three = (rest - two.astype(jnp.float32)).astype(jnp.bfloat16)
    return one.astype(jnp.float32), two.astype(jnp.float32), three.astype(jnp.float32)


def leaf_kernel(tree_ref, sib_ref, near_ref, probes_ref, left_ref, out_ref, one_ref, two_ref):
    spots = (tree_ref[0:3, :] - 4.0) * SQRT_THREE
    norm = spots * spots
    norm = norm[0:1] + norm[1:2] + norm[2:3]
    a, b, c = split_three(spots)
    n1, n2, n3 = split_three(norm)
    unit = jnp.ones_like(norm)
    pad = jnp.zeros((8, LEAF), jnp.float32)
    one_ref[...] = jnp.concatenate(
        [a, a, b, a, c, b, n1, n2, n3, unit, unit, unit, pad], axis=0
    ).astype(jnp.bfloat16)
    two_ref[...] = jnp.concatenate(
        [-2.0 * v for v in (a, b, a, c, a, b)] + [unit, unit, unit, n1, n2, n3, pad], axis=0
    ).astype(jnp.bfloat16)

    levels = left_ref.shape[0]
    left = left_ref[...].reshape(levels * RANK, LEAF)
    out_ref[...] = dot(near_ref[0], left[: 2 * RANK]) + dot(sib_ref[...], left[2 * RANK :])
    eye = lax.broadcasted_iota(jnp.int32, (TILE, TILE), 0) == lax.broadcasted_iota(
        jnp.int32, (TILE, TILE), 1
    )
    tiles = LEAF // TILE
    for i in range(tiles):
        for j in range(i, tiles):
            rows = pl.ds(i * TILE, TILE)
            columns = pl.ds(j * TILE, TILE)
            square = jnp.maximum(dot(one_ref[:, rows], two_ref[:, columns], TN), 1e-30)
            scaled = square * lax.rsqrt(square)
            block = (1.0 + scaled) * jnp.exp(-scaled)
            if i == j:
                block = jnp.where(eye, 1.0 + tree_ref[3:4, rows], block)
            block = block.astype(jnp.bfloat16)
            out_ref[:, columns] += dot(probes_ref[:, rows], block)
            if i != j:
                out_ref[:, rows] += dot(probes_ref[:, columns], block, NT)


def leaves(tree, sib, near, probes, factors):
    points = probes.shape[1]
    levels = factors.shape[0]
    return pl.pallas_call(
        leaf_kernel,
        grid=(points // LEAF,),
        out_shape=jax.ShapeDtypeStruct((PROBES, points), jnp.float32),
        in_specs=[
            pl.BlockSpec((4, LEAF), lambda i: (0, i)),
            pl.BlockSpec(sib.shape, lambda i: (0, 0)),
            pl.BlockSpec((1, PROBES, 2 * RANK), lambda i: (i, 0, 0)),
            pl.BlockSpec((PROBES, LEAF), lambda i: (0, i)),
            pl.BlockSpec((levels, None, RANK, LEAF), lambda i: (0, 0, 0, i)),
        ],
        out_specs=pl.BlockSpec((PROBES, LEAF), lambda i: (0, i)),
        scratch_shapes=[
            pltpu.VMEM((32, LEAF), jnp.bfloat16),
            pltpu.VMEM((32, LEAF), jnp.bfloat16),
        ],
        compiler_params=pltpu.CompilerParams(vmem_limit_bytes=40 * 2**20),
    )(tree, sib, near, probes, factors)


def solution(mesh):
    inner, outer = mesh.shape["gy"], mesh.shape["gx"]

    def local(coords, noise, order, probes, factors):
        tree, sib, near = exchange(inner, outer, coords, noise, order, probes, factors)
        return leaves(tree, sib, near, probes, factors)

    return jax.shard_map(
        local,
        mesh=mesh,
        in_specs=(
            P(None, ("gx", "gy")),
            P(("gx", "gy")),
            P("gx", "gy"),
            P(None, ("gx", "gy")),
            P(None, None, None, ("gx", "gy")),
        ),
        out_specs=P(None, ("gx", "gy")),
        check_vma=False,
    )
```

time: 377 us -> 42.7 us (0.11)
  the two profiles are of different devices: /device:TPU:16 before, /device:TPU:1 now
where the time goes in v1:
time: 42.7 us; the launch traced here: 42.4 us
  Pallas kernels  36.6 us (86%)
  local copies, waits for them, and re-layouts  5.8 us (14%)
    pallas_call x1, Pallas kernels, exchange(): pl.pallas_call(functools.partial(exchange_kernel, inner, outer), out_shap...  27.5 us
    pallas_call x1, Pallas kernels, leaves(): pl.pallas_call(leaf_kernel, grid=(points // LEAF,), out_shape=jax.ShapeDt...  9.06 us
    unnamed x12, local copies, waits for them, and re-layouts  5.8 us

profile of v1, /device:TPU:1, one launch (start us, length us, event | category | flops | bytes accessed | tf_op | source)
XLA Modules:
  0.0 42.4 jit_solution(11478957487871038981)
XLA Ops:
  0.0 0.0 copy-start
  0.0 2.5 %copy-done = bf16[10,2,32,4096]{3,2,1,0:T(8,128)(2,1)S(1)} copy-done((bf16[10,2,32,4096]{3,2,1,0:T(8,128)(2,1)S(1)}, bf16[10,2,32,4096]{3,2,1,0:T(8,128)(2,1)}, u32[]{:S(2)}) %copy-start) | copy-done | bytes 5242904
  2.5 0.0 copy-start.2
  2.5 1.0 %copy-done.2 = bf16[64,4096]{1,0:T(8,128)(2,1)S(1)} copy-done((bf16[64,4096]{1,0:T(8,128)(2,1)S(1)}, bf16[64,4096]{1,0:T(8,128)(2,1)}, u32[]{:S(2)}) %copy-start.2) | copy-done | bytes 524312
  3.5 0.0 copy-start.3
  3.5 0.8 %copy-done.3 = f32[3,4096]{1,0:T(4,128)S(1)} copy-done((f32[3,4096]{1,0:T(4,128)S(1)}, f32[3,4096]{1,0:T(4,128)}, u32[]{:S(2)}) %copy-start.3) | copy-done | bytes 49176
  4.4 0.0 copy-start.4
  4.4 0.7 %copy-done.4 = f32[4096]{0:T(1024)S(1)} copy-done((f32[4096]{0:T(1024)S(1)}, f32[4096]{0:T(1024)}, u32[]{:S(2)}) %copy-start.4) | copy-done | bytes 16408
  5.1 0.0 copy-start.5
  5.1 0.7 %copy-done.5 = s32[1,4096]{1,0:T(1,128)S(1)} copy-done((s32[1,4096]{1,0:T(1,128)S(1)}, s32[1,4096]{1,0:T(1,128)}, u32[]{:S(2)}) %copy-start.5) | copy-done | bytes 16408
  5.8 0.0 copy-start.1
  5.8 27.5 %shard_map.55 = (f32[4,4096]{1,0:T(4,128)S(1)}, bf16[64,256]{1,0:T(8,128)(2,1)S(1)}, bf16[4,64,64]{2,1,0:T(8,128)(2,1)S(1)}) custom-call(f32[3,4096]{1,0:T(4,128)S(1)} %copy-done.3, f32[1,4096]{1,0:T(1,128)S(1)} %bitcast.1, s32[1,4096]{1,0:T(1,128)S(1)} %copy-done.5, bf16[64,4096]{1,0:T(8,128)(2,1)S(1)} %copy-done.2, bf16[10,2,32,4096]{3,2,1,0:T(8,128)(2,1)S(1)} %copy-done), custom_call_target="tpu_custom_call" | custom-call | tf_op jit(solution)/shard_map/pallas_call | solution.py:296
  33.4 0.0 copy-done.1
  33.4 9.1 %shard_map.56 = f32[64,4096]{1,0:T(8,128)} custom-call(f32[4,4096]{1,0:T(4,128)S(1)} %get-tuple-element.8.tree_ref, bf16[64,256]{1,0:T(8,128)(2,1)S(1)} %get-tuple-element.9.sib_ref, bf16[4,64,64]{2,1,0:T(8,128)(2,1)S(1)} %get-tuple-element.10.near_ref, bf16[64,4096]{1,0:T(8,128)(2,1)S(1)} %copy-done.2, bf16[10,2,32,4096]{3,2,1,0:T(8,128)(2,1)S(1)} %copy-done.1), custom_call_target="tpu_custom_call" | custom-call | tf_op jit(solution)/shard_map/pallas_call | solution.py:384
Async XLA Ops:
  0.0 2.5 %copy-start = (bf16[10,2,32,4096]{3,2,1,0:T(8,128)(2,1)S(1)}, bf16[10,2,32,4096]{3,2,1,0:T(8,128)(2,1)}, u32[]{:S(2)}) copy-start(bf16[10,2,32,4096]{3,2,1,0:T(8,128)(2,1)} %left_ref.1) | copy-start | bytes 15728644
  2.5 1.0 %copy-start.2 = (bf16[64,4096]{1,0:T(8,128)(2,1)S(1)}, bf16[64,4096]{1,0:T(8,128)(2,1)}, u32[]{:S(2)}) copy-start(bf16[64,4096]{1,0:T(8,128)(2,1)} %probes_ref.1) | copy-start | bytes 1572868
  3.5 0.8 %copy-start.3 = (f32[3,4096]{1,0:T(4,128)S(1)}, f32[3,4096]{1,0:T(4,128)}, u32[]{:S(2)}) copy-start(f32[3,4096]{1,0:T(4,128)} %coords_hbm.1) | copy-start | bytes 147460
  4.4 0.7 %copy-start.4 = (f32[4096]{0:T(1024)S(1)}, f32[4096]{0:T(1024)}, u32[]{:S(2)}) copy-start(f32[4096]{0:T(1024)} %param.6) | copy-start | bytes 49156
  5.1 0.7 %copy-start.5 = (s32[1,4096]{1,0:T(1,128)S(1)}, s32[1,4096]{1,0:T(1,128)}, u32[]{:S(2)}) copy-start(s32[1,4096]{1,0:T(1,128)} %order_hbm.1) | copy-start | bytes 49156
  5.8 27.6 %copy-start.1 = (bf16[10,2,32,4096]{3,2,1,0:T(8,128)(2,1)S(1)}, bf16[10,2,32,4096]{3,2,1,0:T(8,128)(2,1)}, u32[]{:S(2)}) copy-start(bf16[10,2,32,4096]{3,2,1,0:T(8,128)(2,1)} %left_ref.1) | copy-start | bytes 15728644

commit v2 on v1

--- a/solution.py
+++ b/solution.py
@@ -13,8 +13,8 @@
 LANES = 128
 TILE = 256
 NT = (((1,), (1,)), ((), ()))
-TN = (((0,), (0,)), ((), ()))
 SQRT_THREE = 1.7320508075688772
+LOG2_E = 1.4426950408889634
 
 
 def dot(a, b, dims=(((1,), (0,)), ((), ()))):
@@ -45,6 +45,81 @@
     )
 
 
+def split_three(x):
+    one = x.astype(jnp.bfloat16)
+    rest = x - one.astype(jnp.float32)
+    two = rest.astype(jnp.bfloat16)
+    three = (rest - two.astype(jnp.float32)).astype(jnp.bfloat16)
+    return one.astype(jnp.float32), two.astype(jnp.float32), three.astype(jnp.float32)
+
+
+def far_first(step, size):
+    odd = lax.rem(step, 2)
+    return size // 2 + odd * ((step + 1) // 2) - (1 - odd) * (step // 2)
+
+
+def leaf_features(values):
+    spots = (values[0:3] - 4.0) * SQRT_THREE
+    norm = spots * spots
+    norm = norm[0:1] + norm[1:2] + norm[2:3]
+    a, b, c = split_three(spots)
+    n1, n2, n3 = split_three(norm)
+    unit = jnp.ones_like(norm)
+    pad = jnp.zeros((8, norm.shape[1]), jnp.float32)
+    one = jnp.concatenate([a, a, b, a, c, b, n1, n2, n3, unit, unit, unit, pad], axis=0)
+    two = jnp.concatenate(
+        [-2.0 * v for v in (a, b, a, c, a, b)] + [unit, unit, unit, n1, n2, n3, pad], axis=0
+    )
+    return one.astype(jnp.bfloat16), two.astype(jnp.bfloat16)
+
+
+def matern(square):
+    square = jnp.maximum(square, 1e-30)
+    scaled = square * lax.rsqrt(square)
+    return (1.0 + scaled) * jnp.exp2(scaled * -LOG2_E)
+
+
+def leaf_product(tree, probes, one_ref, two_ref, block_ref, out_ref, start):
+    values = tree[:, pl.ds(start, LEAF)]
+    one, two = leaf_features(values)
+    one_ref[...] = one.T
+    two_ref[...] = two
+    half = TILE // 2
+    eye = lax.broadcasted_iota(jnp.int32, (half, half), 0) == lax.broadcasted_iota(
+        jnp.int32, (half, half), 1
+    )
+    tiles = LEAF // TILE
+    for j in range(tiles):
+        first, middle, last = j * TILE, j * TILE + half, (j + 1) * TILE
+        if j:
+            block_ref[:first, first:last] = matern(
+                dot(one_ref[:first], two_ref[:, first:last])
+            ).astype(jnp.bfloat16)
+        upper = matern(dot(one_ref[first:middle], two_ref[:, first:last]))
+        side = upper[:, half:].astype(jnp.bfloat16)
+        block_ref[first:middle, first:middle] = jnp.where(
+            eye, 1.0 + values[3:4, first:middle], upper[:, :half]
+        ).astype(jnp.bfloat16)
+        block_ref[first:middle, middle:last] = side
+        block_ref[middle:last, first:middle] = side.T
+        block_ref[middle:last, middle:last] = jnp.where(
+            eye,
+            1.0 + values[3:4, middle:last],
+            matern(dot(one_ref[middle:last], two_ref[:, middle:last])),
+        ).astype(jnp.bfloat16)
+    for j in range(tiles):
+        first, last = j * TILE, (j + 1) * TILE
+        columns = pl.ds(start + first, TILE)
+        total = out_ref[:, columns] + dot(
+            probes[:, pl.ds(start, last)], block_ref[:last, first:last]
+        )
+        if j < tiles - 1:
+            total = total + dot(
+                probes[:, pl.ds(start + last, LEAF - last)], block_ref[first:last, last:], NT
+            )
+        out_ref[:, columns] = total
+
+
 def exchange_kernel(
     inner,
     outer,
@@ -53,14 +128,19 @@
     order_hbm,
     probes_hbm,
     factors_hbm,
-    tree_ref,
+    dense_ref,
     sib_ref,
-    near_ref,
+    left_ref,
     coords,
     noise,
     order,
     probes,
     right,
+    beside,
+    tree,
+    one_ref,
+    two_ref,
+    block_ref,
     counts,
     slots,
     table,
@@ -104,11 +184,14 @@
                 (coords_hbm, coords),
                 (noise_hbm, noise),
                 (probes_hbm, probes),
-                (factors_hbm.at[:, 1], right),
+                (factors_hbm.at[2:, 1], right.at[2:]),
+                (factors_hbm.at[:2, 1], right.at[:2]),
+                (factors_hbm.at[:2, 0], beside),
+                (factors_hbm.at[2:, 0], left_ref),
             )
         )
     ]
-    for load in loads:
+    for load in loads[:5]:
         load.start()
 
     def send(step, source, target, axis, peer):
@@ -120,8 +203,8 @@
             device_id={axis: peer},
         ).start()
 
-    def wait_all(sems, step, ref, count):
-        whole = ref.at[pl.ds(0, count)]
+    def wait_all(sems, step, ref, first, count):
+        whole = ref.at[pl.ds(first, count)]
         pltpu.make_async_copy(whole, whole, sems.at[step]).wait()
 
     loads[0].wait()
@@ -163,9 +246,10 @@
 
     pl.semaphore_wait(barrier, inner + outer - 2)
 
-    @pl.loop(1, inner)
-    def _(j):
-        send(0, ask.at[j], asked.at[j - 1], "gy", lax.rem(gy + j, inner))
+    @pl.loop(0, inner - 1)
+    def _(step):
+        j = far_first(step, inner)
+        send(0, ask.at[j], asked.at[j], "gy", lax.rem(gy + j, inner))
 
     loads[3].wait()
     loads[4].wait()
@@ -175,11 +259,13 @@
         part[k] = coeff[k * share : (k + 1) * share]
     parts[pl.ds(gy, 1)] = part[pl.ds(gy, 1)]
 
-    @pl.loop(1, inner)
-    def _(j):
-        peer = lax.rem(gy + j, inner)
+    @pl.loop(0, inner - 1)
+    def _(step):
+        peer = lax.rem(gy + far_first(step, inner), inner)
         send(2, part.at[peer], parts.at[gy], "gy", peer)
 
+    for load in loads[5:]:
+        load.start()
     loads[1].wait()
     loads[2].wait()
     values = jnp.concatenate([coords[...], noise[...]], axis=0)
@@ -192,6 +278,10 @@
     for r in range(points // TILE):
         table[r] = vectors_own[r]
 
+    given[0] = look_up(vectors_own, ask[0, 0:1], ask[0, 1:2])
+
+    loads[5].wait()
+    loads[6].wait()
     near = [
         dot(
             vectors[:, a * LEAF : (a + 1) * LEAF],
@@ -203,22 +293,23 @@
     level = lax.broadcasted_iota(jnp.int32, (PROBES, 2 * RANK), 1) < RANK
     for a in range(points // LEAF):
         other = 2 * (1 - a // 2)
-        near_ref[a] = jnp.where(level, near[a ^ 1], near[other] + near[other + 1]).astype(
-            jnp.bfloat16
-        )
-
-    own_table = [table[r] for r in range(points // TILE)]
-    given[0] = look_up(own_table, ask[0, 0:1], ask[0, 1:2])
-    wait_all(recv_sem, 0, asked, inner - 1)
-
-    @pl.loop(1, inner)
-    def _(j):
+        sibling = jnp.where(level, near[a ^ 1], near[other] + near[other + 1])
+        dense_ref[:, a * LEAF : (a + 1) * LEAF] = dot(
+            sibling.astype(jnp.bfloat16),
+            beside[:, :, a * LEAF : (a + 1) * LEAF].reshape(2 * RANK, LEAF),
+        )
+
+    wait_all(recv_sem, 0, asked, 1, inner - 1)
+
+    @pl.loop(0, inner - 1)
+    def _(step):
+        j = far_first(step, inner)
         own_table = [table[r] for r in range(points // TILE)]
-        lists = asked[j - 1]
-        give[j - 1] = look_up(own_table, lists[0:1], lists[1:2])
-        send(1, give.at[j - 1], given.at[j], "gy", lax.rem(gy - j + inner, inner))
-
-    wait_all(recv_sem, 2, parts, inner - 1)
+        lists = asked[j]
+        give[j] = look_up(own_table, lists[0:1], lists[1:2])
+        send(1, give.at[j], given.at[j], "gy", lax.rem(gy - j + inner, inner))
+
+    wait_all(recv_sem, 2, parts, 0, inner - 1)
     half = inner_bits * RANK
     lane = lax.broadcasted_iota(jnp.int32, (share, half), 1)
     sums = [[parts[e] for e in range(inner)]]
@@ -238,18 +329,7 @@
             picked = jnp.where(lane < (h + 1) * RANK, sums[h][(d >> h) ^ 1][:, :half], picked)
         inner_sib[d] = picked
 
-    wait_all(recv_sem, 1, given, inner - 1)
-    received = [given[r] for r in range(inner)]
-    for k in range(chunks):
-        found = look_up(
-            received,
-            slots[:, 2 * k * LANES : (2 * k + 1) * LANES],
-            slots[:, (2 * k + 1) * LANES : (2 * k + 2) * LANES],
-        )
-        tree_ref[:, 2 * k * LANES : (2 * k + 1) * LANES] = found[0:4]
-        tree_ref[:, (2 * k + 1) * LANES : (2 * k + 2) * LANES] = found[4:8]
-
-    wait_all(recv_sem, 3, totals, outer - 1)
+    wait_all(recv_sem, 3, totals, 0, outer - 1)
     width = outer_bits * RANK
     lane = lax.broadcasted_iota(jnp.int32, (share, width), 1)
     base = 0
@@ -267,19 +347,43 @@
         back[d] = jnp.concatenate([inner_sib[d], picked], axis=1)
     backs[pl.ds(gy, 1)] = back[pl.ds(gy, 1)]
 
-    @pl.loop(1, inner)
-    def _(j):
-        peer = lax.rem(gy + j, inner)
+    @pl.loop(0, inner - 1)
+    def _(step):
+        peer = lax.rem(gy + far_first(step, inner), inner)
         send(4, back.at[peer], backs.at[gy], "gy", peer)
 
-    wait_all(recv_sem, 4, backs, inner - 1)
+    wait_all(recv_sem, 1, given, 1, inner - 1)
+    received = [given[r] for r in range(inner)]
+    for k in range(chunks):
+        found = look_up(
+            received,
+            slots[:, 2 * k * LANES : (2 * k + 1) * LANES],
+            slots[:, (2 * k + 1) * LANES : (2 * k + 2) * LANES],
+        )
+        tree[:, 2 * k * LANES : (2 * k + 1) * LANES] = found[0:4]
+        tree[:, (2 * k + 1) * LANES : (2 * k + 2) * LANES] = found[4:8]
+
+    @pl.loop(0, points // LEAF)
+    def _(a):
+        leaf_product(
+            tree,
+            probes,
+            one_ref,
+            two_ref,
+            block_ref,
+            dense_ref,
+            pl.multiple_of(a * LEAF, LEAF),
+        )
+
+    wait_all(recv_sem, 4, backs, 0, inner - 1)
     sib_ref[...] = jnp.concatenate([backs[k] for k in range(inner)], axis=0).astype(jnp.bfloat16)
 
-    wait_all(send_sem, 0, asked, inner - 1)
-    wait_all(send_sem, 1, give, inner - 1)
-    wait_all(send_sem, 2, part, inner - 1)
-    wait_all(send_sem, 3, totals, outer - 1)
-    wait_all(send_sem, 4, back, inner - 1)
+    loads[7].wait()
+    wait_all(send_sem, 0, ask, 1, inner - 1)
+    wait_all(send_sem, 1, give, 1, inner - 1)
+    wait_all(send_sem, 2, part, 0, inner - 1)
+    wait_all(send_sem, 3, totals, 0, outer - 1)
+    wait_all(send_sem, 4, back, 0, inner - 1)
 
 
 def exchange(inner, outer, coords, noise, order, probes, factors):
@@ -291,14 +395,14 @@
     outer_bits = outer.bit_length() - 1
     wide = far * RANK
     f32, bf16, i32 = jnp.float32, jnp.bfloat16, jnp.int32
-    hbm = pl.BlockSpec(memory_space=pl.ANY)
+    hbm = pl.BlockSpec(memory_space=pltpu.HBM)
     vmem = pl.BlockSpec(memory_space=pltpu.VMEM)
     return pl.pallas_call(
         functools.partial(exchange_kernel, inner, outer),
         out_shape=(
-            jax.ShapeDtypeStruct((4, points), f32),
+            jax.ShapeDtypeStruct((PROBES, points), f32),
             jax.ShapeDtypeStruct((PROBES, wide), bf16),
-            jax.ShapeDtypeStruct((points // LEAF, PROBES, 2 * RANK), bf16),
+            jax.ShapeDtypeStruct((far, RANK, points), bf16),
         ),
         in_specs=[hbm] * 5,
         out_specs=(vmem, vmem, vmem),
@@ -308,12 +412,17 @@
             pltpu.VMEM((1, points), i32),
             pltpu.VMEM((PROBES, points), bf16),
             pltpu.VMEM((levels, RANK, points), bf16),
+            pltpu.VMEM((2, RANK, points), bf16),
+            pltpu.VMEM((4, points), f32),
+            pltpu.VMEM((LEAF, 32), bf16),
+            pltpu.VMEM((32, LEAF), bf16),
+            pltpu.VMEM((LEAF, LEAF), bf16),
             pltpu.VMEM((inner * points // TILE, TILE), bf16),
             pltpu.VMEM((1, points), i32),
             pltpu.VMEM((points // TILE, 8, LANES), f32),
             pltpu.VMEM((inner, 2, LANES), i32),
-            pltpu.VMEM((inner - 1, 2, LANES), i32),
-            pltpu.VMEM((inner - 1, 8, LANES), f32),
+            pltpu.VMEM((inner, 2, LANES), i32),
+            pltpu.VMEM((inner, 8, LANES), f32),
             pltpu.VMEM((inner, 8, LANES), f32),
             pltpu.VMEM((inner, share, wide), f32),
             pltpu.VMEM((inner, share, wide), f32),
@@ -323,90 +432,60 @@
             pltpu.VMEM((2 * outer, share, outer_bits * RANK), f32),
             pltpu.VMEM((inner, share, wide), f32),
             pltpu.VMEM((inner, share, wide), f32),
-            pltpu.SemaphoreType.DMA((5,)),
+            pltpu.SemaphoreType.DMA((8,)),
             pltpu.SemaphoreType.DMA((5,)),
             pltpu.SemaphoreType.DMA((5,)),
         ],
         compiler_params=pltpu.CompilerParams(
             collective_id=0, has_side_effects=True, vmem_limit_bytes=40 * 2**20
         ),
-    )(coords, noise.reshape(1, points), order, probes, factors)
-
-
-def split_three(x):
-    one = x.astype(jnp.bfloat16)
-    rest = x - one.astype(jnp.float32)
-    two = rest.astype(jnp.bfloat16)
-    three = (rest - two.astype(jnp.float32)).astype(jnp.bfloat16)
-    return one.astype(jnp.float32), two.astype(jnp.float32), three.astype(jnp.float32)
-
-
-def leaf_kernel(tree_ref, sib_ref, near_ref, probes_ref, left_ref, out_ref, one_ref, two_ref):
-    spots = (tree_ref[0:3, :] - 4.0) * SQRT_THREE
-    norm = spots * spots
-    norm = norm[0:1] + norm[1:2] + norm[2:3]
-    a, b, c = split_three(spots)
-    n1, n2, n3 = split_three(norm)
-    unit = jnp.ones_like(norm)
-    pad = jnp.zeros((8, LEAF), jnp.float32)
-    one_ref[...] = jnp.concatenate(
-        [a, a, b, a, c, b, n1, n2, n3, unit, unit, unit, pad], axis=0
-    ).astype(jnp.bfloat16)
-    two_ref[...] = jnp.concatenate(
-        [-2.0 * v for v in (a, b, a, c, a, b)] + [unit, unit, unit, n1, n2, n3, pad], axis=0
-    ).astype(jnp.bfloat16)
-
-    levels = left_ref.shape[0]
-    left = left_ref[...].reshape(levels * RANK, LEAF)
-    out_ref[...] = dot(near_ref[0], left[: 2 * RANK]) + dot(sib_ref[...], left[2 * RANK :])
-    eye = lax.broadcasted_iota(jnp.int32, (TILE, TILE), 0) == lax.broadcasted_iota(
-        jnp.int32, (TILE, TILE), 1
+    )(
+        *(
+            pltpu.with_memory_space_constraint(array, pltpu.HBM)
+            for array in (coords, noise.reshape(1, points), order, probes, factors)
+        )
     )
-    tiles = LEAF // TILE
-    for i in range(tiles):
-        for j in range(i, tiles):
-            rows = pl.ds(i * TILE, TILE)
-            columns = pl.ds(j * TILE, TILE)
-            square = jnp.maximum(dot(one_ref[:, rows], two_ref[:, columns], TN), 1e-30)
-            scaled = square * lax.rsqrt(square)
-            block = (1.0 + scaled) * jnp.exp(-scaled)
-            if i == j:
-                block = jnp.where(eye, 1.0 + tree_ref[3:4, rows], block)
-            block = block.astype(jnp.bfloat16)
-            out_ref[:, columns] += dot(probes_ref[:, rows], block)
-            if i != j:
-                out_ref[:, rows] += dot(probes_ref[:, columns], block, NT)
-
-
-def leaves(tree, sib, near, probes, factors):
-    points = probes.shape[1]
-    levels = factors.shape[0]
+
+
+def expand_kernel(dense, sib, left, out_hbm, result, sems):
+    points = dense.shape[1]
+    width = result.shape[2]
+    writes = []
+    for c in range(points // width):
+        columns = slice(c * width, (c + 1) * width)
+        result[c] = dense[:, columns] + dot(
+            sib[...], left[:, :, columns].reshape(sib.shape[1], width)
+        )
+        writes.append(
+            pltpu.make_async_copy(result.at[c], out_hbm.at[:, columns], sems.at[c])
+        )
+        writes[-1].start()
+    for write in writes:
+        write.wait()
+
+
+def expand(dense, sib, left):
+    points = dense.shape[1]
+    width = 512
+    vmem = pl.BlockSpec(memory_space=pltpu.VMEM)
     return pl.pallas_call(
-        leaf_kernel,
-        grid=(points // LEAF,),
+        expand_kernel,
         out_shape=jax.ShapeDtypeStruct((PROBES, points), jnp.float32),
-        in_specs=[
-            pl.BlockSpec((4, LEAF), lambda i: (0, i)),
-            pl.BlockSpec(sib.shape, lambda i: (0, 0)),
-            pl.BlockSpec((1, PROBES, 2 * RANK), lambda i: (i, 0, 0)),
-            pl.BlockSpec((PROBES, LEAF), lambda i: (0, i)),
-            pl.BlockSpec((levels, None, RANK, LEAF), lambda i: (0, 0, 0, i)),
+        in_specs=[vmem] * 3,
+        out_specs=pl.BlockSpec(memory_space=pltpu.HBM),
+        scratch_shapes=[
+            pltpu.VMEM((points // width, PROBES, width), jnp.float32),
+            pltpu.SemaphoreType.DMA((points // width,)),
         ],
-        out_specs=pl.BlockSpec((PROBES, LEAF), lambda i: (0, i)),
-        scratch_shapes=[
-            pltpu.VMEM((32, LEAF), jnp.bfloat16),
-            pltpu.VMEM((32, LEAF), jnp.bfloat16),
-        ],
-        compiler_params=pltpu.CompilerParams(vmem_limit_bytes=40 * 2**20),
-    )(tree, sib, near, probes, factors)
+        compiler_params=pltpu.CompilerParams(vmem_limit_bytes=16 * 2**20),
+    )(dense, sib, left)
 
 
 def solution(mesh):
     inner, outer = mesh.shape["gy"], mesh.shape["gx"]
 
     def local(coords, noise, order, probes, factors):
-        tree, sib, near = exchange(inner, outer, coords, noise, order, probes, factors)
-        return leaves(tree, sib, near, probes, factors)
+        return expand(*exchange(inner, outer, coords, noise, order, probes, factors))
 
     return jax.shard_map(
         local,

time: 42.7 us -> 28.2 us (0.66)
  Pallas kernels: 36.6 us -> 28 us
  local copies, waits for them, and re-layouts: 5.8 us -> 0 us
    pallas_call x1, Pallas kernels: 9.06 us -> 1.25 us  [expand(): pl.pallas_call(expand_kernel, out_shape=jax.ShapeDtypeStruct((PROBES, poi...]
    unnamed x12 -> x0, local copies, waits for them, and re-layouts: 5.8 us -> none
    pallas_call x1, Pallas kernels: 27.5 us -> 26.8 us  [exchange(): pl.pallas_call(functools.partial(exchange_kernel, inner, outer), out_shap...]
where the time goes in v2:
time: 28.2 us; the launch traced here: 28 us
  Pallas kernels  28 us (99%)
    pallas_call x1, Pallas kernels, exchange(): pl.pallas_call(functools.partial(exchange_kernel, inner, outer), out_shap...  26.8 us
    pallas_call x1, Pallas kernels, expand(): pl.pallas_call(expand_kernel, out_shape=jax.ShapeDtypeStruct((PROBES, poi...  1.25 us

profile of v2, /device:TPU:1, one launch (start us, length us, event | category | flops | bytes accessed | tf_op | source)
XLA Modules:
  0.0 28.0 jit_solution(7639609873204406834)
XLA Ops:
  0.0 26.8 %shard_map.55 = (f32[64,4096]{1,0:T(8,128)S(1)}, bf16[64,256]{1,0:T(8,128)(2,1)S(1)}, bf16[8,32,4096]{2,1,0:T(8,128)(2,1)S(1)}) custom-call(f32[3,4096]{1,0:T(4,128)} %coords_hbm.1, f32[1,4096]{1,0:T(1,128)} %bitcast.1, s32[1,4096]{1,0:T(1,128)} %order_hbm.1, bf16[64,4096]{1,0:T(8,128)(2,1)} %probes_hbm.1, bf16[10,2,32,4096]{3,2,1,0:T(8,128)(2,1)} %factors_hbm.1), custom_call_target="tpu_custom_call" | custom-call | tf_op jit(solution)/shard_map/pallas_call | solution.py:400
  26.8 1.2 %shard_map.56 = f32[64,4096]{1,0:T(8,128)} custom-call(f32[64,4096]{1,0:T(8,128)S(1)} %get-tuple-element.8.dense, bf16[64,256]{1,0:T(8,128)(2,1)S(1)} %get-tuple-element.9.sib, bf16[8,32,4096]{2,1,0:T(8,128)(2,1)S(1)} %get-tuple-element.10.left), custom_call_target="tpu_custom_call" | custom-call | tf_op jit(solution)/shard_map/pallas_call | solution.py:471

commit v3 on v2

--- a/solution.py
+++ b/solution.py
@@ -12,6 +12,7 @@
 PROBES = 64
 LANES = 128
 TILE = 256
+OWNERS = 8
 NT = (((1,), (1,)), ((), ()))
 SQRT_THREE = 1.7320508075688772
 LOG2_E = 1.4426950408889634
@@ -74,23 +75,47 @@
 
 
 def matern(square):
-    square = jnp.maximum(square, 1e-30)
-    scaled = square * lax.rsqrt(square)
+    scaled = square * lax.rsqrt(jnp.maximum(square, 1e-3))
     return (1.0 + scaled) * jnp.exp2(scaled * -LOG2_E)
 
 
-def leaf_product(tree, probes, one_ref, two_ref, block_ref, out_ref, start):
-    values = tree[:, pl.ds(start, LEAF)]
-    one, two = leaf_features(values)
-    one_ref[...] = one.T
-    two_ref[...] = two
+def leaf_products(given, slots, probes, even, odd, out_ref):
+    points = slots.shape[1]
     half = TILE // 2
-    eye = lax.broadcasted_iota(jnp.int32, (half, half), 0) == lax.broadcasted_iota(
-        jnp.int32, (half, half), 1
-    )
     tiles = LEAF // TILE
-    for j in range(tiles):
+
+    def multiply(leaf, block_ref):
+        start = leaf * LEAF
+        for j in range(tiles):
+            first, last = j * TILE, (j + 1) * TILE
+            columns = pl.ds(pl.multiple_of(start + first, TILE), TILE)
+            total = out_ref[:, columns] + dot(
+                probes[:, pl.ds(pl.multiple_of(start, TILE), last)], block_ref[:last, first:last]
+            )
+            if j < tiles - 1:
+                rest = pl.ds(pl.multiple_of(start + last, TILE), LEAF - last)
+                total = total + dot(probes[:, rest], block_ref[first:last, last:], NT)
+            out_ref[:, columns] = total
+
+    def find(leaf, j, noise_ref, one_ref, two_ref, block_ref):
+        at = leaf * LEAF + j * TILE
+        found = look_up(
+            [given[r] for r in range(given.shape[0])],
+            slots[:, pl.ds(pl.multiple_of(at, LANES), LANES)],
+            slots[:, pl.ds(pl.multiple_of(at + LANES, LANES), LANES)],
+        )
+        columns = slice(j * TILE, (j + 1) * TILE)
+        values = jnp.concatenate([found[0:4], found[4:8]], axis=1)
+        one, two = leaf_features(values)
+        one_ref[columns, :] = one.T
+        two_ref[:, columns] = two
+        noise_ref[:, columns] = 1.0 + values[3:4]
+
+    def fill(j, noise_ref, one_ref, two_ref, block_ref):
         first, middle, last = j * TILE, j * TILE + half, (j + 1) * TILE
+        eye = lax.broadcasted_iota(jnp.int32, (half, half), 0) == lax.broadcasted_iota(
+            jnp.int32, (half, half), 1
+        )
         if j:
             block_ref[:first, first:last] = matern(
                 dot(one_ref[:first], two_ref[:, first:last])
@@ -98,26 +123,28 @@
         upper = matern(dot(one_ref[first:middle], two_ref[:, first:last]))
         side = upper[:, half:].astype(jnp.bfloat16)
         block_ref[first:middle, first:middle] = jnp.where(
-            eye, 1.0 + values[3:4, first:middle], upper[:, :half]
+            eye, noise_ref[:, first:middle], upper[:, :half]
         ).astype(jnp.bfloat16)
         block_ref[first:middle, middle:last] = side
         block_ref[middle:last, first:middle] = side.T
         block_ref[middle:last, middle:last] = jnp.where(
             eye,
-            1.0 + values[3:4, middle:last],
+            noise_ref[:, middle:last],
             matern(dot(one_ref[middle:last], two_ref[:, middle:last])),
         ).astype(jnp.bfloat16)
+
+    leaves = points // LEAF
+
+    sets = (even, odd)
     for j in range(tiles):
-        first, last = j * TILE, (j + 1) * TILE
-        columns = pl.ds(start + first, TILE)
-        total = out_ref[:, columns] + dot(
-            probes[:, pl.ds(start, last)], block_ref[:last, first:last]
-        )
-        if j < tiles - 1:
-            total = total + dot(
-                probes[:, pl.ds(start + last, LEAF - last)], block_ref[first:last, last:], NT
-            )
-        out_ref[:, columns] = total
+        find(0, j, *even)
+    for leaf in range(leaves):
+        now, later = sets[leaf % 2], sets[(leaf + 1) % 2]
+        for j in range(tiles):
+            fill(j, *now)
+            if leaf + 1 < leaves:
+                find(leaf + 1, j, *later)
+        multiply(leaf, now[3])
 
 
 def exchange_kernel(
@@ -137,10 +164,8 @@
     probes,
     right,
     beside,
-    tree,
-    one_ref,
-    two_ref,
-    block_ref,
+    even,
+    odd,
     counts,
     slots,
     table,
@@ -150,12 +175,15 @@
     given,
     part,
     parts,
-    inner_sib,
+    outer_part,
+    outer_parts,
     total,
     totals,
     pairs,
     back,
     backs,
+    outer_back,
+    outer_backs,
     load_sem,
     send_sem,
     recv_sem,
@@ -168,6 +196,9 @@
     inner_bits = inner.bit_length() - 1
     outer_bits = outer.bit_length() - 1
     share = PROBES // inner
+    owner_share = PROBES // OWNERS
+    half = inner_bits * RANK
+    owner = gy < OWNERS
 
     barrier = pltpu.get_barrier_semaphore()
     for axis, own, size in (("gy", gy, inner), ("gx", gx, outer)):
@@ -244,20 +275,32 @@
     for j in range(inner):
         ask[j] = lists[2 * j : 2 * j + 2]
 
-    pl.semaphore_wait(barrier, inner + outer - 2)
-
-    @pl.loop(0, inner - 1)
-    def _(step):
-        j = far_first(step, inner)
-        send(0, ask.at[j], asked.at[j], "gy", lax.rem(gy + j, inner))
-
     loads[3].wait()
     loads[4].wait()
     vectors = probes[...]
     coeff = dot(vectors, right[2:].reshape(far * RANK, points), NT)
+    for k in range(OWNERS):
+        outer_part[k] = coeff[k * owner_share : (k + 1) * owner_share, half:]
     for k in range(inner):
-        part[k] = coeff[k * share : (k + 1) * share]
+        part[k] = coeff[k * share : (k + 1) * share, :half]
     parts[pl.ds(gy, 1)] = part[pl.ds(gy, 1)]
+
+    pl.semaphore_wait(barrier, inner + outer - 2)
+
+    @pl.loop(0, inner - 1, unroll=True)
+    def _(step):
+        j = far_first(step, inner)
+        send(0, ask.at[j], asked.at[j], "gy", lax.rem(gy + j, inner))
+
+    @pl.loop(0, OWNERS)
+    def _(k):
+        @pl.when(k != gy)
+        def _():
+            send(3, outer_part.at[k], outer_parts.at[gy], "gy", k)
+
+    @pl.when(owner)
+    def _():
+        outer_parts[pl.ds(gy, 1)] = outer_part[pl.ds(gy, 1)]
 
     @pl.loop(0, inner - 1)
     def _(step):
@@ -299,6 +342,19 @@
             beside[:, :, a * LEAF : (a + 1) * LEAF].reshape(2 * RANK, LEAF),
         )
 
+    @pl.when(owner)
+    def _():
+        wait_all(recv_sem, 3, outer_parts, 0, inner - 1)
+        sums = [outer_parts[e] for e in range(inner)]
+        while len(sums) > 1:
+            sums = [sums[2 * g] + sums[2 * g + 1] for g in range(len(sums) // 2)]
+        total[...] = sums[0]
+        totals[pl.ds(gx, 1)] = sums[0][None]
+
+        @pl.loop(1, outer, unroll=True)
+        def _(j):
+            send(4, total, totals.at[gx], "gx", lax.rem(gx + j, outer))
+
     wait_all(recv_sem, 0, asked, 1, inner - 1)
 
     @pl.loop(0, inner - 1)
@@ -310,80 +366,82 @@
         send(1, give.at[j], given.at[j], "gy", lax.rem(gy - j + inner, inner))
 
     wait_all(recv_sem, 2, parts, 0, inner - 1)
-    half = inner_bits * RANK
     lane = lax.broadcasted_iota(jnp.int32, (share, half), 1)
     sums = [[parts[e] for e in range(inner)]]
-    for step in range(inner_bits):
+    for step in range(inner_bits - 1):
         last = sums[-1]
         sums.append([last[2 * g] + last[2 * g + 1] for g in range(len(last) // 2)])
-    total[...] = sums[inner_bits][0][:, half:]
-    totals[pl.ds(gx, 1)] = total[...][None]
-
-    @pl.loop(1, outer)
-    def _(j):
-        send(3, total, totals.at[gx], "gx", lax.rem(gx + j, outer))
-
     for d in range(inner):
-        picked = sums[inner_bits - 1][(d >> (inner_bits - 1)) ^ 1][:, :half]
+        picked = sums[inner_bits - 1][(d >> (inner_bits - 1)) ^ 1]
         for h in reversed(range(inner_bits - 1)):
-            picked = jnp.where(lane < (h + 1) * RANK, sums[h][(d >> h) ^ 1][:, :half], picked)
-        inner_sib[d] = picked
-
-    wait_all(recv_sem, 3, totals, 0, outer - 1)
-    width = outer_bits * RANK
-    lane = lax.broadcasted_iota(jnp.int32, (share, width), 1)
-    base = 0
-    sums = [totals[e] for e in range(outer)]
-    picked = None
-    for h in range(outer_bits):
-        for g, value in enumerate(sums):
-            pairs[base + g] = value
-        group = gx // 2**h
-        sibling = pairs[base + group + 1 - 2 * (group % 2)]
-        picked = sibling if picked is None else jnp.where(lane < h * RANK, picked, sibling)
-        base += len(sums)
-        sums = [sums[2 * g] + sums[2 * g + 1] for g in range(len(sums) // 2)]
-    for d in range(inner):
-        back[d] = jnp.concatenate([inner_sib[d], picked], axis=1)
+            picked = jnp.where(lane < (h + 1) * RANK, sums[h][(d >> h) ^ 1], picked)
+        back[d] = picked
     backs[pl.ds(gy, 1)] = back[pl.ds(gy, 1)]
 
     @pl.loop(0, inner - 1)
     def _(step):
         peer = lax.rem(gy + far_first(step, inner), inner)
-        send(4, back.at[peer], backs.at[gy], "gy", peer)
+        send(5, back.at[peer], backs.at[gy], "gy", peer)
+
+    @pl.when(owner)
+    def _():
+        wait_all(recv_sem, 4, totals, 0, outer - 1)
+        width = outer_bits * RANK
+        lane = lax.broadcasted_iota(jnp.int32, (owner_share, width), 1)
+        base = 0
+        sums = [totals[e] for e in range(outer)]
+        picked = None
+        for h in range(outer_bits):
+            for g, value in enumerate(sums):
+                pairs[base + g] = value
+            group = gx // 2**h
+            sibling = pairs[base + group + 1 - 2 * (group % 2)]
+            picked = sibling if picked is None else jnp.where(lane < h * RANK, picked, sibling)
+            base += len(sums)
+            sums = [sums[2 * g] + sums[2 * g + 1] for g in range(len(sums) // 2)]
+        outer_back[...] = picked
+        outer_backs[pl.ds(gy, 1)] = picked[None]
+
+        @pl.loop(1, inner, unroll=True)
+        def _(j):
+            send(6, outer_back, outer_backs.at[gy], "gy", lax.rem(gy + j, inner))
 
     wait_all(recv_sem, 1, given, 1, inner - 1)
-    received = [given[r] for r in range(inner)]
-    for k in range(chunks):
-        found = look_up(
-            received,
-            slots[:, 2 * k * LANES : (2 * k + 1) * LANES],
-            slots[:, (2 * k + 1) * LANES : (2 * k + 2) * LANES],
-        )
-        tree[:, 2 * k * LANES : (2 * k + 1) * LANES] = found[0:4]
-        tree[:, (2 * k + 1) * LANES : (2 * k + 2) * LANES] = found[4:8]
-
-    @pl.loop(0, points // LEAF)
-    def _(a):
-        leaf_product(
-            tree,
-            probes,
-            one_ref,
-            two_ref,
-            block_ref,
-            dense_ref,
-            pl.multiple_of(a * LEAF, LEAF),
-        )
-
-    wait_all(recv_sem, 4, backs, 0, inner - 1)
-    sib_ref[...] = jnp.concatenate([backs[k] for k in range(inner)], axis=0).astype(jnp.bfloat16)
+    leaf_products(given, slots, probes, even, odd, dense_ref)
+
+    wait_all(recv_sem, 5, backs, 0, inner - 1)
+
+    @pl.when(owner)
+    def _():
+        wait_all(recv_sem, 6, outer_backs, 0, OWNERS - 1)
+
+    @pl.when(jnp.logical_not(owner))
+    def _():
+        wait_all(recv_sem, 6, outer_backs, 0, OWNERS)
+
+    sib_ref[...] = jnp.concatenate(
+        [
+            jnp.concatenate([backs[k] for k in range(inner)], axis=0),
+            jnp.concatenate([outer_backs[k] for k in range(OWNERS)], axis=0),
+        ],
+        axis=1,
+    ).astype(jnp.bfloat16)
 
     loads[7].wait()
     wait_all(send_sem, 0, ask, 1, inner - 1)
     wait_all(send_sem, 1, give, 1, inner - 1)
     wait_all(send_sem, 2, part, 0, inner - 1)
-    wait_all(send_sem, 3, totals, 0, outer - 1)
-    wait_all(send_sem, 4, back, 0, inner - 1)
+    wait_all(send_sem, 5, back, 0, inner - 1)
+
+    @pl.when(owner)
+    def _():
+        wait_all(send_sem, 3, outer_part, 0, OWNERS - 1)
+        wait_all(send_sem, 4, totals, 0, outer - 1)
+        wait_all(send_sem, 6, outer_parts, 0, inner - 1)
+
+    @pl.when(jnp.logical_not(owner))
+    def _():
+        wait_all(send_sem, 3, outer_part, 0, OWNERS)
 
 
 def exchange(inner, outer, coords, noise, order, probes, factors):
@@ -391,11 +449,18 @@
     levels = factors.shape[0]
     far = levels - 2
     share = PROBES // inner
+    owner_share = PROBES // OWNERS
     inner_bits = inner.bit_length() - 1
     outer_bits = outer.bit_length() - 1
     wide = far * RANK
     f32, bf16, i32 = jnp.float32, jnp.bfloat16, jnp.int32
     hbm = pl.BlockSpec(memory_space=pltpu.HBM)
+    leaf_set = (
+        pltpu.VMEM((1, LEAF), f32),
+        pltpu.VMEM((LEAF, 32), bf16),
+        pltpu.VMEM((32, LEAF), bf16),
+        pltpu.VMEM((LEAF, LEAF), bf16),
+    )
     vmem = pl.BlockSpec(memory_space=pltpu.VMEM)
     return pl.pallas_call(
         functools.partial(exchange_kernel, inner, outer),
@@ -413,10 +478,8 @@
             pltpu.VMEM((PROBES, points), bf16),
             pltpu.VMEM((levels, RANK, points), bf16),
             pltpu.VMEM((2, RANK, points), bf16),
-            pltpu.VMEM((4, points), f32),
-            pltpu.VMEM((LEAF, 32), bf16),
-            pltpu.VMEM((32, LEAF), bf16),
-            pltpu.VMEM((LEAF, LEAF), bf16),
+            leaf_set,
+            leaf_set,
             pltpu.VMEM((inner * points // TILE, TILE), bf16),
             pltpu.VMEM((1, points), i32),
             pltpu.VMEM((points // TILE, 8, LANES), f32),
@@ -424,17 +487,20 @@
             pltpu.VMEM((inner, 2, LANES), i32),
             pltpu.VMEM((inner, 8, LANES), f32),
             pltpu.VMEM((inner, 8, LANES), f32),
-            pltpu.VMEM((inner, share, wide), f32),
-            pltpu.VMEM((inner, share, wide), f32),
             pltpu.VMEM((inner, share, inner_bits * RANK), f32),
-            pltpu.VMEM((share, outer_bits * RANK), f32),
-            pltpu.VMEM((outer, share, outer_bits * RANK), f32),
-            pltpu.VMEM((2 * outer, share, outer_bits * RANK), f32),
-            pltpu.VMEM((inner, share, wide), f32),
-            pltpu.VMEM((inner, share, wide), f32),
+            pltpu.VMEM((inner, share, inner_bits * RANK), f32),
+            pltpu.VMEM((OWNERS, owner_share, outer_bits * RANK), f32),
+            pltpu.VMEM((inner, owner_share, outer_bits * RANK), f32),
+            pltpu.VMEM((owner_share, outer_bits * RANK), f32),
+            pltpu.VMEM((outer, owner_share, outer_bits * RANK), f32),
+            pltpu.VMEM((2 * outer, owner_share, outer_bits * RANK), f32),
+            pltpu.VMEM((inner, share, inner_bits * RANK), f32),
+            pltpu.VMEM((inner, share, inner_bits * RANK), f32),
+            pltpu.VMEM((owner_share, outer_bits * RANK), f32),
+            pltpu.VMEM((OWNERS, owner_share, outer_bits * RANK), f32),
             pltpu.SemaphoreType.DMA((8,)),
-            pltpu.SemaphoreType.DMA((5,)),
-            pltpu.SemaphoreType.DMA((5,)),
+            pltpu.SemaphoreType.DMA((7,)),
+            pltpu.SemaphoreType.DMA((7,)),
         ],
         compiler_params=pltpu.CompilerParams(
             collective_id=0, has_side_effects=True, vmem_limit_bytes=40 * 2**20

time: 28.2 us -> 27.4 us (0.972)
  Pallas kernels: 28 us -> 27.2 us
    pallas_call x1, Pallas kernels: 26.8 us -> 26 us  [exchange(): pl.pallas_call(functools.partial(exchange_kernel, inner, outer), out_shap...]
where the time goes in v3:
time: 27.4 us; the launch traced here: 27.2 us
  Pallas kernels  27.2 us (99%)
    pallas_call x1, Pallas kernels, exchange(): pl.pallas_call(functools.partial(exchange_kernel, inner, outer), out_shap...  26 us
    pallas_call x1, Pallas kernels, expand(): pl.pallas_call(expand_kernel, out_shape=jax.ShapeDtypeStruct((PROBES, poi...  1.25 us

profile of v3, /device:TPU:1, one launch (start us, length us, event | category | flops | bytes accessed | tf_op | source)
XLA Modules:
  0.0 27.2 jit_solution(15204865371678782005)
XLA Ops:
  0.0 26.0 %shard_map.55 = (f32[64,4096]{1,0:T(8,128)S(1)}, bf16[64,256]{1,0:T(8,128)(2,1)S(1)}, bf16[8,32,4096]{2,1,0:T(8,128)(2,1)S(1)}) custom-call(f32[3,4096]{1,0:T(4,128)} %coords_hbm.1, f32[1,4096]{1,0:T(1,128)} %bitcast.1, s32[1,4096]{1,0:T(1,128)} %order_hbm.1, bf16[64,4096]{1,0:T(8,128)(2,1)} %probes_hbm.1, bf16[10,2,32,4096]{3,2,1,0:T(8,128)(2,1)} %factors_hbm.1), custom_call_target="tpu_custom_call" | custom-call | tf_op jit(solution)/shard_map/pallas_call | solution.py:465
  26.0 1.2 %shard_map.56 = f32[64,4096]{1,0:T(8,128)} custom-call(f32[64,4096]{1,0:T(8,128)S(1)} %get-tuple-element.8.dense, bf16[64,256]{1,0:T(8,128)(2,1)S(1)} %get-tuple-element.9.sib, bf16[8,32,4096]{2,1,0:T(8,128)(2,1)S(1)} %get-tuple-element.10.left), custom_call_target="tpu_custom_call" | custom-call | tf_op jit(solution)/shard_map/pallas_call | solution.py:537

commit v4 on v3

--- a/solution.py
+++ b/solution.py
@@ -28,15 +28,15 @@
     for picks in (first, second):
         picks = jnp.broadcast_to(picks, shape)
         lane = picks & (LANES - 1)
-        upper = picks >> 8
-        out = jnp.zeros(shape, jnp.float32)
-        for r, vector in enumerate(table):
-            out = jnp.where(
-                upper == r,
-                jnp.take_along_axis(vector, lane, axis=1, mode="promise_in_bounds"),
-                out,
-            )
-        found.append((out, ((picks >> 7) & 1) == 0))
+        out = [
+            jnp.take_along_axis(vector, lane, axis=1, mode="promise_in_bounds") for vector in table
+        ]
+        bit = 8
+        while len(out) > 1:
+            odd = ((picks >> bit) & 1) == 1
+            out = [jnp.where(odd, out[g + 1], out[g]) for g in range(0, len(out), 2)]
+            bit += 1
+        found.append((out[0], ((picks >> 7) & 1) == 0))
     row = lax.broadcasted_iota(jnp.int32, shape, 0)
     (one, one_low), (two, two_low) = found
     return jnp.where(
@@ -84,18 +84,29 @@
     half = TILE // 2
     tiles = LEAF // TILE
 
-    def multiply(leaf, block_ref):
+    def multiply(leaf, j, block_ref):
         start = leaf * LEAF
-        for j in range(tiles):
-            first, last = j * TILE, (j + 1) * TILE
-            columns = pl.ds(pl.multiple_of(start + first, TILE), TILE)
-            total = out_ref[:, columns] + dot(
-                probes[:, pl.ds(pl.multiple_of(start, TILE), last)], block_ref[:last, first:last]
+        first, last = j * TILE, (j + 1) * TILE
+        columns = slice(start + first, start + last)
+        total = out_ref[:, columns] + dot(
+            probes[:, start : start + last], block_ref[:last, first:last]
+        )
+        if j < tiles - 1:
+            total = total + dot(
+                probes[:, start + last : start + LEAF], block_ref[first:last, last:], NT
             )
-            if j < tiles - 1:
-                rest = pl.ds(pl.multiple_of(start + last, TILE), LEAF - last)
-                total = total + dot(probes[:, rest], block_ref[first:last, last:], NT)
-            out_ref[:, columns] = total
+        out_ref[:, columns] = total
+
+    def multiply_now(leaf, j, block_ref):
+        start = leaf * LEAF
+        first, last = j * TILE, (j + 1) * TILE
+        columns = slice(start + first, start + last)
+        out_ref[:, columns] += dot(probes[:, start : start + last], block_ref[:last, first:last])
+        for i in range(j):
+            before = slice(start + i * TILE, start + (i + 1) * TILE)
+            out_ref[:, before] += dot(
+                probes[:, columns], block_ref[i * TILE : (i + 1) * TILE, first:last], NT
+            )
 
     def find(leaf, j, noise_ref, one_ref, two_ref, block_ref):
         at = leaf * LEAF + j * TILE
@@ -139,12 +150,15 @@
     for j in range(tiles):
         find(0, j, *even)
     for leaf in range(leaves):
-        now, later = sets[leaf % 2], sets[(leaf + 1) % 2]
+        now, other = sets[leaf % 2], sets[(leaf + 1) % 2]
         for j in range(tiles):
             fill(j, *now)
+            if leaf:
+                multiply(leaf - 1, j, other[3])
             if leaf + 1 < leaves:
-                find(leaf + 1, j, *later)
-        multiply(leaf, now[3])
+                find(leaf + 1, j, *other)
+    for j in range(tiles):
+        multiply(leaves - 1, j, sets[(leaves - 1) % 2][3])
 
 
 def exchange_kernel(
@@ -184,6 +198,7 @@
     backs,
     outer_back,
     outer_backs,
+    ready,
     load_sem,
     send_sem,
     recv_sem,
@@ -195,50 +210,102 @@
     far = levels - 2
     inner_bits = inner.bit_length() - 1
     outer_bits = outer.bit_length() - 1
-    share = PROBES // inner
-    owner_share = PROBES // OWNERS
+    share = PROBES // OWNERS
+    late = inner - OWNERS
     half = inner_bits * RANK
     owner = gy < OWNERS
 
-    barrier = pltpu.get_barrier_semaphore()
-    for axis, own, size in (("gy", gy, inner), ("gx", gx, outer)):
-
-        @pl.loop(1, size)
-        def _(j):
-            pl.semaphore_signal(barrier, inc=1, device_id={axis: lax.rem(own + j, size)})
-
+    outer_first = levels - outer_bits
     loads = [
         pltpu.make_async_copy(source, target, load_sem.at[i])
         for i, (source, target) in enumerate(
             (
+                (probes_hbm, probes),
+                (factors_hbm.at[outer_first:, 1], right.at[outer_first:]),
                 (order_hbm, order),
                 (coords_hbm, coords),
                 (noise_hbm, noise),
-                (probes_hbm, probes),
-                (factors_hbm.at[2:, 1], right.at[2:]),
+                (factors_hbm.at[2:outer_first, 1], right.at[2:outer_first]),
                 (factors_hbm.at[:2, 1], right.at[:2]),
                 (factors_hbm.at[:2, 0], beside),
                 (factors_hbm.at[2:, 0], left_ref),
             )
         )
     ]
-    for load in loads[:5]:
+    for load in loads[:6]:
         load.start()
 
-    def send(step, source, target, axis, peer):
+    barrier = pltpu.get_barrier_semaphore()
+
+    @pl.when(owner)
+    def _():
+        @pl.loop(0, inner - 1)
+        def _(step):
+            peer = lax.rem(gy + far_first(step, inner), inner)
+            pl.semaphore_signal(barrier, inc=1, device_id={"gy": peer})
+
+        @pl.loop(0, outer - 1)
+        def _(step):
+            peer = lax.rem(gx + far_first(step, outer), outer)
+            pl.semaphore_signal(barrier, inc=1, device_id={"gx": peer})
+
+    @pl.when(jnp.logical_not(owner))
+    def _():
+        pl.semaphore_wait(barrier, OWNERS)
+
+        @pl.loop(0, OWNERS)
+        def _(k):
+            pl.semaphore_signal(ready, inc=1, device_id={"gy": k})
+
+    def send(step, source, target, axis, peer, arrival=None):
         pltpu.make_async_remote_copy(
             src_ref=source,
             dst_ref=target,
             send_sem=send_sem.at[step],
-            recv_sem=recv_sem.at[step],
+            recv_sem=recv_sem.at[step if arrival is None else arrival],
             device_id={axis: peer},
         ).start()
+
+    def others(first, last, body):
+        @pl.loop(first, last)
+        def _(k):
+            pl.when(k != gy)(lambda: body(k))
+
+    def request(arrival):
+        def to(k):
+            j = lax.rem(k - gy + inner, inner)
+            send(0, ask.at[j], asked.at[j], "gy", k, arrival)
+
+        return to
+
+    def give_part(k):
+        send(3, outer_part.at[k], outer_parts.at[gy], "gy", k)
+
+    def give_inner_part(k):
+        send(2, part.at[k], parts.at[gy], "gy", k)
+
+    def answer(j):
+        own_table = [table[r] for r in range(points // TILE)]
+        lists = asked[j]
+        give[j] = look_up(own_table, lists[0:1], lists[1:2])
+        send(1, give.at[j], given.at[j], "gy", lax.rem(gy - j + inner, inner))
 
     def wait_all(sems, step, ref, first, count):
         whole = ref.at[pl.ds(first, count)]
         pltpu.make_async_copy(whole, whole, sems.at[step]).wait()
 
     loads[0].wait()
+    loads[1].wait()
+    vectors = probes[...]
+    coeff = dot(vectors, right[outer_first:].reshape(outer_bits * RANK, points), NT)
+    for k in range(OWNERS):
+        outer_part[k] = coeff[k * share : (k + 1) * share]
+
+    @pl.when(jnp.logical_not(owner))
+    def _():
+        others(0, OWNERS, give_part)
+
+    loads[2].wait()
     wanted = order[...]
     source = ((wanted >> (points.bit_length() - 1)) - gy) & (inner - 1)
     local_index = wanted & (points - 1)
@@ -275,42 +342,24 @@
     for j in range(inner):
         ask[j] = lists[2 * j : 2 * j + 2]
 
+    @pl.when(jnp.logical_not(owner))
+    def _():
+        others(0, OWNERS, request(7))
+
+    loads[5].wait()
+    coeff = dot(vectors, right[2:outer_first].reshape(inner_bits * RANK, points), NT)
+    for k in range(OWNERS):
+        part[k] = coeff[k * share : (k + 1) * share]
+
+    @pl.when(jnp.logical_not(owner))
+    def _():
+        others(0, OWNERS, give_inner_part)
+
+    for load in loads[6:]:
+        load.start()
+
     loads[3].wait()
     loads[4].wait()
-    vectors = probes[...]
-    coeff = dot(vectors, right[2:].reshape(far * RANK, points), NT)
-    for k in range(OWNERS):
-        outer_part[k] = coeff[k * owner_share : (k + 1) * owner_share, half:]
-    for k in range(inner):
-        part[k] = coeff[k * share : (k + 1) * share, :half]
-    parts[pl.ds(gy, 1)] = part[pl.ds(gy, 1)]
-
-    pl.semaphore_wait(barrier, inner + outer - 2)
-
-    @pl.loop(0, inner - 1, unroll=True)
-    def _(step):
-        j = far_first(step, inner)
-        send(0, ask.at[j], asked.at[j], "gy", lax.rem(gy + j, inner))
-
-    @pl.loop(0, OWNERS)
-    def _(k):
-        @pl.when(k != gy)
-        def _():
-            send(3, outer_part.at[k], outer_parts.at[gy], "gy", k)
-
-    @pl.when(owner)
-    def _():
-        outer_parts[pl.ds(gy, 1)] = outer_part[pl.ds(gy, 1)]
-
-    @pl.loop(0, inner - 1)
-    def _(step):
-        peer = lax.rem(gy + far_first(step, inner), inner)
-        send(2, part.at[peer], parts.at[gy], "gy", peer)
-
-    for load in loads[5:]:
-        load.start()
-    loads[1].wait()
-    loads[2].wait()
     values = jnp.concatenate([coords[...], noise[...]], axis=0)
     vectors_own = [
         jnp.concatenate(
@@ -321,10 +370,21 @@
     for r in range(points // TILE):
         table[r] = vectors_own[r]
 
+    @pl.when(owner)
+    def _():
+        parts[pl.ds(gy, 1)] = part[pl.ds(gy, 1)]
+        outer_parts[pl.ds(gy, 1)] = outer_part[pl.ds(gy, 1)]
+        pl.semaphore_wait(barrier, OWNERS - 1 + outer - 1)
+        others(0, OWNERS, give_part)
+        others(0, OWNERS, request(0))
+        pl.semaphore_wait(ready, late)
+        others(OWNERS, inner, request(0))
+        others(0, OWNERS, give_inner_part)
+
     given[0] = look_up(vectors_own, ask[0, 0:1], ask[0, 1:2])
 
-    loads[5].wait()
     loads[6].wait()
+    loads[7].wait()
     near = [
         dot(
             vectors[:, a * LEAF : (a + 1) * LEAF],
@@ -351,43 +411,49 @@
         total[...] = sums[0]
         totals[pl.ds(gx, 1)] = sums[0][None]
 
-        @pl.loop(1, outer, unroll=True)
-        def _(j):
-            send(4, total, totals.at[gx], "gx", lax.rem(gx + j, outer))
-
-    wait_all(recv_sem, 0, asked, 1, inner - 1)
-
-    @pl.loop(0, inner - 1)
-    def _(step):
-        j = far_first(step, inner)
-        own_table = [table[r] for r in range(points // TILE)]
-        lists = asked[j]
-        give[j] = look_up(own_table, lists[0:1], lists[1:2])
-        send(1, give.at[j], given.at[j], "gy", lax.rem(gy - j + inner, inner))
-
-    wait_all(recv_sem, 2, parts, 0, inner - 1)
-    lane = lax.broadcasted_iota(jnp.int32, (share, half), 1)
-    sums = [[parts[e] for e in range(inner)]]
-    for step in range(inner_bits - 1):
-        last = sums[-1]
-        sums.append([last[2 * g] + last[2 * g + 1] for g in range(len(last) // 2)])
-    for d in range(inner):
-        picked = sums[inner_bits - 1][(d >> (inner_bits - 1)) ^ 1]
-        for h in reversed(range(inner_bits - 1)):
-            picked = jnp.where(lane < (h + 1) * RANK, sums[h][(d >> h) ^ 1], picked)
-        back[d] = picked
-    backs[pl.ds(gy, 1)] = back[pl.ds(gy, 1)]
-
-    @pl.loop(0, inner - 1)
-    def _(step):
-        peer = lax.rem(gy + far_first(step, inner), inner)
-        send(5, back.at[peer], backs.at[gy], "gy", peer)
+        @pl.loop(0, outer - 1, unroll=True)
+        def _(step):
+            peer = lax.rem(gx + far_first(step, outer), outer)
+            send(4, total, totals.at[gx], "gx", peer)
+
+    @pl.when(owner)
+    def _():
+        wait_all(recv_sem, 7, asked, 0, late)
+        wait_all(recv_sem, 0, asked, 0, OWNERS - 1)
+
+        @pl.loop(0, inner - 1)
+        def _(step):
+            answer(far_first(step, inner))
+
+    @pl.when(jnp.logical_not(owner))
+    def _():
+        wait_all(recv_sem, 0, asked, 0, OWNERS)
+        others(0, OWNERS, lambda k: answer(lax.rem(gy - k + inner, inner)))
+        others(OWNERS, inner, request(7))
+        wait_all(recv_sem, 7, asked, 0, late - 1)
+        others(OWNERS, inner, lambda k: answer(lax.rem(gy - k + inner, inner)))
+
+    @pl.when(owner)
+    def _():
+        wait_all(recv_sem, 2, parts, 0, inner - 1)
+        lane = lax.broadcasted_iota(jnp.int32, (share, half), 1)
+        sums = [[parts[e] for e in range(inner)]]
+        for step in range(inner_bits - 1):
+            last = sums[-1]
+            sums.append([last[2 * g] + last[2 * g + 1] for g in range(len(last) // 2)])
+        for d in range(inner):
+            picked = sums[inner_bits - 1][(d >> (inner_bits - 1)) ^ 1]
+            for h in reversed(range(inner_bits - 1)):
+                picked = jnp.where(lane < (h + 1) * RANK, sums[h][(d >> h) ^ 1], picked)
+            back[d] = picked
+        backs[pl.ds(gy, 1)] = back[pl.ds(gy, 1)]
+        others(0, inner, lambda k: send(5, back.at[k], backs.at[gy], "gy", k))
 
     @pl.when(owner)
     def _():
         wait_all(recv_sem, 4, totals, 0, outer - 1)
         width = outer_bits * RANK
-        lane = lax.broadcasted_iota(jnp.int32, (owner_share, width), 1)
+        lane = lax.broadcasted_iota(jnp.int32, (share, width), 1)
         base = 0
         sums = [totals[e] for e in range(outer)]
         picked = None
@@ -402,45 +468,41 @@
         outer_back[...] = picked
         outer_backs[pl.ds(gy, 1)] = picked[None]
 
-        @pl.loop(1, inner, unroll=True)
-        def _(j):
-            send(6, outer_back, outer_backs.at[gy], "gy", lax.rem(gy + j, inner))
+        others(0, inner, lambda k: send(6, outer_back, outer_backs.at[gy], "gy", k))
 
     wait_all(recv_sem, 1, given, 1, inner - 1)
     leaf_products(given, slots, probes, even, odd, dense_ref)
 
-    wait_all(recv_sem, 5, backs, 0, inner - 1)
-
-    @pl.when(owner)
-    def _():
+    @pl.when(owner)
+    def _():
+        wait_all(recv_sem, 5, backs, 0, OWNERS - 1)
         wait_all(recv_sem, 6, outer_backs, 0, OWNERS - 1)
 
     @pl.when(jnp.logical_not(owner))
     def _():
+        wait_all(recv_sem, 5, backs, 0, OWNERS)
         wait_all(recv_sem, 6, outer_backs, 0, OWNERS)
 
-    sib_ref[...] = jnp.concatenate(
-        [
-            jnp.concatenate([backs[k] for k in range(inner)], axis=0),
-            jnp.concatenate([outer_backs[k] for k in range(OWNERS)], axis=0),
-        ],
-        axis=1,
-    ).astype(jnp.bfloat16)
-
-    loads[7].wait()
+    for k in range(OWNERS):
+        sib_ref[k * share : (k + 1) * share, :] = jnp.concatenate(
+            [backs[k], outer_backs[k]], axis=1
+        )
+
+    loads[8].wait()
     wait_all(send_sem, 0, ask, 1, inner - 1)
     wait_all(send_sem, 1, give, 1, inner - 1)
-    wait_all(send_sem, 2, part, 0, inner - 1)
-    wait_all(send_sem, 5, back, 0, inner - 1)
-
-    @pl.when(owner)
-    def _():
+
+    @pl.when(owner)
+    def _():
+        wait_all(send_sem, 2, part, 0, OWNERS - 1)
         wait_all(send_sem, 3, outer_part, 0, OWNERS - 1)
         wait_all(send_sem, 4, totals, 0, outer - 1)
+        wait_all(send_sem, 5, back, 0, inner - 1)
         wait_all(send_sem, 6, outer_parts, 0, inner - 1)
 
     @pl.when(jnp.logical_not(owner))
     def _():
+        wait_all(send_sem, 2, part, 0, OWNERS)
         wait_all(send_sem, 3, outer_part, 0, OWNERS)
 
 
@@ -448,8 +510,7 @@
     points = probes.shape[1]
     levels = factors.shape[0]
     far = levels - 2
-    share = PROBES // inner
-    owner_share = PROBES // OWNERS
+    share = PROBES // OWNERS
     inner_bits = inner.bit_length() - 1
     outer_bits = outer.bit_length() - 1
     wide = far * RANK
@@ -466,7 +527,7 @@
         functools.partial(exchange_kernel, inner, outer),
         out_shape=(
             jax.ShapeDtypeStruct((PROBES, points), f32),
-            jax.ShapeDtypeStruct((PROBES, wide), bf16),
+            jax.ShapeDtypeStruct((PROBES, wide), f32),
             jax.ShapeDtypeStruct((far, RANK, points), bf16),
         ),
         in_specs=[hbm] * 5,
@@ -487,20 +548,21 @@
             pltpu.VMEM((inner, 2, LANES), i32),
             pltpu.VMEM((inner, 8, LANES), f32),
             pltpu.VMEM((inner, 8, LANES), f32),
+            pltpu.VMEM((OWNERS, share, inner_bits * RANK), f32),
             pltpu.VMEM((inner, share, inner_bits * RANK), f32),
+            pltpu.VMEM((OWNERS, share, outer_bits * RANK), f32),
+            pltpu.VMEM((inner, share, outer_bits * RANK), f32),
+            pltpu.VMEM((share, outer_bits * RANK), f32),
+            pltpu.VMEM((outer, share, outer_bits * RANK), f32),
+            pltpu.VMEM((2 * outer, share, outer_bits * RANK), f32),
             pltpu.VMEM((inner, share, inner_bits * RANK), f32),
-            pltpu.VMEM((OWNERS, owner_share, outer_bits * RANK), f32),
-            pltpu.VMEM((inner, owner_share, outer_bits * RANK), f32),
-            pltpu.VMEM((owner_share, outer_bits * RANK), f32),
-            pltpu.VMEM((outer, owner_share, outer_bits * RANK), f32),
-            pltpu.VMEM((2 * outer, owner_share, outer_bits * RANK), f32),
-            pltpu.VMEM((inner, share, inner_bits * RANK), f32),
-            pltpu.VMEM((inner, share, inner_bits * RANK), f32),
-            pltpu.VMEM((owner_share, outer_bits * RANK), f32),
-            pltpu.VMEM((OWNERS, owner_share, outer_bits * RANK), f32),
+            pltpu.VMEM((OWNERS, share, inner_bits * RANK), f32),
+            pltpu.VMEM((share, outer_bits * RANK), f32),
+            pltpu.VMEM((OWNERS, share, outer_bits * RANK), f32),
+            pltpu.SemaphoreType.REGULAR,
+            pltpu.SemaphoreType.DMA((9,)),
+            pltpu.SemaphoreType.DMA((7,)),
             pltpu.SemaphoreType.DMA((8,)),
-            pltpu.SemaphoreType.DMA((7,)),
-            pltpu.SemaphoreType.DMA((7,)),
         ],
         compiler_params=pltpu.CompilerParams(
             collective_id=0, has_side_effects=True, vmem_limit_bytes=40 * 2**20
@@ -517,10 +579,11 @@
     points = dense.shape[1]
     width = result.shape[2]
     writes = []
+    rounded = sib[...].astype(jnp.bfloat16)
     for c in range(points // width):
         columns = slice(c * width, (c + 1) * width)
         result[c] = dense[:, columns] + dot(
-            sib[...], left[:, :, columns].reshape(sib.shape[1], width)
+            rounded, left[:, :, columns].reshape(sib.shape[1], width)
         )
         writes.append(
             pltpu.make_async_copy(result.at[c], out_hbm.at[:, columns], sems.at[c])

time: 27.4 us -> 25.1 us (0.916)
  Pallas kernels: 27.2 us -> 24.9 us
    pallas_call x1, Pallas kernels: 26 us -> 23.7 us  [exchange(): pl.pallas_call(functools.partial(exchange_kernel, inner, outer), out_shap...]
where the time goes in v4:
time: 25.1 us; the launch traced here: 25 us
  Pallas kernels  24.9 us (99%)
    pallas_call x1, Pallas kernels, exchange(): pl.pallas_call(functools.partial(exchange_kernel, inner, outer), out_shap...  23.7 us
    pallas_call x1, Pallas kernels, expand(): pl.pallas_call(expand_kernel, out_shape=jax.ShapeDtypeStruct((PROBES, poi...  1.24 us

profile of v4, /device:TPU:1, one launch (start us, length us, event | category | flops | bytes accessed | tf_op | source)
XLA Modules:
  0.0 25.0 jit_solution(11314228482150638978)
XLA Ops:
  0.0 23.7 %shard_map.55 = (f32[64,4096]{1,0:T(8,128)S(1)}, f32[64,256]{1,0:T(8,128)S(1)}, bf16[8,32,4096]{2,1,0:T(8,128)(2,1)S(1)}) custom-call(f32[3,4096]{1,0:T(4,128)} %coords_hbm.1, f32[1,4096]{1,0:T(1,128)} %bitcast.1, s32[1,4096]{1,0:T(1,128)} %order_hbm.1, bf16[64,4096]{1,0:T(8,128)(2,1)} %probes_hbm.1, bf16[10,2,32,4096]{3,2,1,0:T(8,128)(2,1)} %factors_hbm.1), custom_call_target="tpu_custom_call" | custom-call | tf_op jit(solution)/shard_map/pallas_call | solution.py:526
  23.7 1.2 %shard_map.56 = f32[64,4096]{1,0:T(8,128)} custom-call(f32[64,4096]{1,0:T(8,128)S(1)} %get-tuple-element.8.dense, f32[64,256]{1,0:T(8,128)S(1)} %get-tuple-element.9.sib, bf16[8,32,4096]{2,1,0:T(8,128)(2,1)S(1)} %get-tuple-element.10.left), custom_call_target="tpu_custom_call" | custom-call | tf_op jit(solution)/shard_map/pallas_call | solution.py:600

commit v5 on v4

--- a/solution.py
+++ b/solution.py
@@ -199,6 +199,7 @@
     outer_back,
     outer_backs,
     ready,
+    everyone,
     load_sem,
     send_sem,
     recv_sem,
@@ -216,24 +217,30 @@
     owner = gy < OWNERS
 
     outer_first = levels - outer_bits
+    runs = [slice(a * LEAF, (a + 1) * LEAF) for a in range(points // LEAF)]
+    pieces = []
+    for run in runs:
+        pieces.append((probes_hbm.at[:, run], probes.at[:, run]))
+        pieces.append((factors_hbm.at[outer_first:, 1, :, run], right.at[outer_first:, :, run]))
+    pieces += [
+        (order_hbm, order),
+        (coords_hbm, coords),
+        (noise_hbm, noise),
+        (factors_hbm.at[2:outer_first, 1], right.at[2:outer_first]),
+        (factors_hbm.at[:2, 1], right.at[:2]),
+        (factors_hbm.at[:2, 0], beside),
+        (factors_hbm.at[2:, 0], left_ref),
+    ]
+    early = 2 * len(runs) + 4
     loads = [
         pltpu.make_async_copy(source, target, load_sem.at[i])
-        for i, (source, target) in enumerate(
-            (
-                (probes_hbm, probes),
-                (factors_hbm.at[outer_first:, 1], right.at[outer_first:]),
-                (order_hbm, order),
-                (coords_hbm, coords),
-                (noise_hbm, noise),
-                (factors_hbm.at[2:outer_first, 1], right.at[2:outer_first]),
-                (factors_hbm.at[:2, 1], right.at[:2]),
-                (factors_hbm.at[:2, 0], beside),
-                (factors_hbm.at[2:, 0], left_ref),
-            )
-        )
+        for i, (source, target) in enumerate(pieces)
     ]
-    for load in loads[:6]:
+    for load in loads[:early]:
         load.start()
+    order_load, coords_load, noise_load, inner_load, near_load, beside_load, *rest_loads = loads[
+        2 * len(runs) :
+    ]
 
     barrier = pltpu.get_barrier_semaphore()
 
@@ -268,7 +275,8 @@
 
     def others(first, last, body):
         @pl.loop(first, last)
-        def _(k):
+        def _(step):
+            k = step + 1 - 2 * lax.rem(step, 2)
             pl.when(k != gy)(lambda: body(k))
 
     def request(arrival):
@@ -294,10 +302,13 @@
         whole = ref.at[pl.ds(first, count)]
         pltpu.make_async_copy(whole, whole, sems.at[step]).wait()
 
-    loads[0].wait()
-    loads[1].wait()
-    vectors = probes[...]
-    coeff = dot(vectors, right[outer_first:].reshape(outer_bits * RANK, points), NT)
+    coeff = 0.0
+    for a, run in enumerate(runs):
+        loads[2 * a].wait()
+        loads[2 * a + 1].wait()
+        coeff = coeff + dot(
+            probes[:, run], right[outer_first:, :, run].reshape(outer_bits * RANK, LEAF), NT
+        )
     for k in range(OWNERS):
         outer_part[k] = coeff[k * share : (k + 1) * share]
 
@@ -305,7 +316,7 @@
     def _():
         others(0, OWNERS, give_part)
 
-    loads[2].wait()
+    order_load.wait()
     wanted = order[...]
     source = ((wanted >> (points.bit_length() - 1)) - gy) & (inner - 1)
     local_index = wanted & (points - 1)
@@ -346,7 +357,8 @@
     def _():
         others(0, OWNERS, request(7))
 
-    loads[5].wait()
+    inner_load.wait()
+    vectors = probes[...]
     coeff = dot(vectors, right[2:outer_first].reshape(inner_bits * RANK, points), NT)
     for k in range(OWNERS):
         part[k] = coeff[k * share : (k + 1) * share]
@@ -355,11 +367,11 @@
     def _():
         others(0, OWNERS, give_inner_part)
 
-    for load in loads[6:]:
+    for load in loads[early:]:
         load.start()
 
-    loads[3].wait()
-    loads[4].wait()
+    coords_load.wait()
+    noise_load.wait()
     values = jnp.concatenate([coords[...], noise[...]], axis=0)
     vectors_own = [
         jnp.concatenate(
@@ -379,12 +391,21 @@
         others(0, OWNERS, request(0))
         pl.semaphore_wait(ready, late)
         others(OWNERS, inner, request(0))
+
+        for teller, first in ((OWNERS - 1, OWNERS), (0, OWNERS + late // 2)):
+
+            @pl.when(gy == teller)
+            def _():
+                @pl.loop(first, first + late // 2)
+                def _(k):
+                    pl.semaphore_signal(everyone, inc=1, device_id={"gy": k})
+
         others(0, OWNERS, give_inner_part)
 
     given[0] = look_up(vectors_own, ask[0, 0:1], ask[0, 1:2])
 
-    loads[6].wait()
-    loads[7].wait()
+    near_load.wait()
+    beside_load.wait()
     near = [
         dot(
             vectors[:, a * LEAF : (a + 1) * LEAF],
@@ -427,9 +448,10 @@
 
     @pl.when(jnp.logical_not(owner))
     def _():
+        pl.semaphore_wait(everyone, 1)
+        others(OWNERS, inner, request(7))
         wait_all(recv_sem, 0, asked, 0, OWNERS)
         others(0, OWNERS, lambda k: answer(lax.rem(gy - k + inner, inner)))
-        others(OWNERS, inner, request(7))
         wait_all(recv_sem, 7, asked, 0, late - 1)
         others(OWNERS, inner, lambda k: answer(lax.rem(gy - k + inner, inner)))
 
@@ -488,7 +510,8 @@
             [backs[k], outer_backs[k]], axis=1
         )
 
-    loads[8].wait()
+    for load in rest_loads:
+        load.wait()
     wait_all(send_sem, 0, ask, 1, inner - 1)
     wait_all(send_sem, 1, give, 1, inner - 1)
 
@@ -560,7 +583,8 @@
             pltpu.VMEM((share, outer_bits * RANK), f32),
             pltpu.VMEM((OWNERS, share, outer_bits * RANK), f32),
             pltpu.SemaphoreType.REGULAR,
-            pltpu.SemaphoreType.DMA((9,)),
+            pltpu.SemaphoreType.REGULAR,
+            pltpu.SemaphoreType.DMA((2 * (points // LEAF) + 7,)),
             pltpu.SemaphoreType.DMA((7,)),
             pltpu.SemaphoreType.DMA((8,)),
         ],

time: 25.1 us -> 24.9 us (level)
  no operation moved by 1% of the time
where the time goes in v5:
time: 24.9 us; the launch traced here: 24.8 us
  Pallas kernels  24.8 us (100%)
    pallas_call x1, Pallas kernels, exchange(): pl.pallas_call(functools.partial(exchange_kernel, inner, outer), out_shap...  23.5 us
    pallas_call x1, Pallas kernels, expand(): pl.pallas_call(expand_kernel, out_shape=jax.ShapeDtypeStruct((PROBES, poi...  1.25 us

profile of v5, /device:TPU:1, one launch (start us, length us, event | category | flops | bytes accessed | tf_op | source)
XLA Modules:
  0.0 24.8 jit_solution(10101493827698504885)
XLA Ops:
  0.0 23.5 %shard_map.55 = (f32[64,4096]{1,0:T(8,128)S(1)}, f32[64,256]{1,0:T(8,128)S(1)}, bf16[8,32,4096]{2,1,0:T(8,128)(2,1)S(1)}) custom-call(f32[3,4096]{1,0:T(4,128)} %coords_hbm.1, f32[1,4096]{1,0:T(1,128)} %bitcast.1, s32[1,4096]{1,0:T(1,128)} %order_hbm.1, bf16[64,4096]{1,0:T(8,128)(2,1)} %probes_hbm.1, bf16[10,2,32,4096]{3,2,1,0:T(8,128)(2,1)} %factors_hbm.1), custom_call_target="tpu_custom_call" | custom-call | tf_op jit(solution)/shard_map/pallas_call | solution.py:549
  23.5 1.2 %shard_map.56 = f32[64,4096]{1,0:T(8,128)} custom-call(f32[64,4096]{1,0:T(8,128)S(1)} %get-tuple-element.8.dense, f32[64,256]{1,0:T(8,128)S(1)} %get-tuple-element.9.sib, bf16[8,32,4096]{2,1,0:T(8,128)(2,1)S(1)} %get-tuple-element.10.left), custom_call_target="tpu_custom_call" | custom-call | tf_op jit(solution)/shard_map/pallas_call | solution.py:624

commit v6 on v5

--- a/solution.py
+++ b/solution.py
@@ -96,17 +96,6 @@
                 probes[:, start + last : start + LEAF], block_ref[first:last, last:], NT
             )
         out_ref[:, columns] = total
-
-    def multiply_now(leaf, j, block_ref):
-        start = leaf * LEAF
-        first, last = j * TILE, (j + 1) * TILE
-        columns = slice(start + first, start + last)
-        out_ref[:, columns] += dot(probes[:, start : start + last], block_ref[:last, first:last])
-        for i in range(j):
-            before = slice(start + i * TILE, start + (i + 1) * TILE)
-            out_ref[:, before] += dot(
-                probes[:, columns], block_ref[i * TILE : (i + 1) * TILE, first:last], NT
-            )
 
     def find(leaf, j, noise_ref, one_ref, two_ref, block_ref):
         at = leaf * LEAF + j * TILE
@@ -314,7 +303,8 @@
 
     @pl.when(jnp.logical_not(owner))
     def _():
-        others(0, OWNERS, give_part)
+        for k in range(OWNERS):
+            give_part(k)
 
     order_load.wait()
     wanted = order[...]
@@ -467,7 +457,7 @@
             picked = sums[inner_bits - 1][(d >> (inner_bits - 1)) ^ 1]
             for h in reversed(range(inner_bits - 1)):
                 picked = jnp.where(lane < (h + 1) * RANK, sums[h][(d >> h) ^ 1], picked)
-            back[d] = picked
+            back[d] = picked.astype(jnp.bfloat16)
         backs[pl.ds(gy, 1)] = back[pl.ds(gy, 1)]
         others(0, inner, lambda k: send(5, back.at[k], backs.at[gy], "gy", k))
 
@@ -487,10 +477,14 @@
             picked = sibling if picked is None else jnp.where(lane < h * RANK, picked, sibling)
             base += len(sums)
             sums = [sums[2 * g] + sums[2 * g + 1] for g in range(len(sums) // 2)]
-        outer_back[...] = picked
-        outer_backs[pl.ds(gy, 1)] = picked[None]
-
-        others(0, inner, lambda k: send(6, outer_back, outer_backs.at[gy], "gy", k))
+        rounded = picked.astype(jnp.bfloat16)[None]
+        outer_back[...] = rounded
+        outer_backs[pl.ds(gy, 1)] = rounded
+
+
+        @pl.loop(1, inner, unroll=True)
+        def _(j):
+            send(6, outer_back.at[0], outer_backs.at[gy], "gy", lax.rem(gy - j + inner, inner))
 
     wait_all(recv_sem, 1, given, 1, inner - 1)
     leaf_products(given, slots, probes, even, odd, dense_ref)
@@ -508,7 +502,7 @@
     for k in range(OWNERS):
         sib_ref[k * share : (k + 1) * share, :] = jnp.concatenate(
             [backs[k], outer_backs[k]], axis=1
-        )
+        ).astype(jnp.float32)
 
     for load in rest_loads:
         load.wait()
@@ -521,7 +515,7 @@
         wait_all(send_sem, 3, outer_part, 0, OWNERS - 1)
         wait_all(send_sem, 4, totals, 0, outer - 1)
         wait_all(send_sem, 5, back, 0, inner - 1)
-        wait_all(send_sem, 6, outer_parts, 0, inner - 1)
+        wait_all(send_sem, 6, back, 0, inner - 1)
 
     @pl.when(jnp.logical_not(owner))
     def _():
@@ -578,10 +572,10 @@
             pltpu.VMEM((share, outer_bits * RANK), f32),
             pltpu.VMEM((outer, share, outer_bits * RANK), f32),
             pltpu.VMEM((2 * outer, share, outer_bits * RANK), f32),
-            pltpu.VMEM((inner, share, inner_bits * RANK), f32),
-            pltpu.VMEM((OWNERS, share, inner_bits * RANK), f32),
-            pltpu.VMEM((share, outer_bits * RANK), f32),
-            pltpu.VMEM((OWNERS, share, outer_bits * RANK), f32),
+            pltpu.VMEM((inner, share, inner_bits * RANK), bf16),
+            pltpu.VMEM((OWNERS, share, inner_bits * RANK), bf16),
+            pltpu.VMEM((1, share, outer_bits * RANK), bf16),
+            pltpu.VMEM((OWNERS, share, outer_bits * RANK), bf16),
             pltpu.SemaphoreType.REGULAR,
             pltpu.SemaphoreType.REGULAR,
             pltpu.SemaphoreType.DMA((2 * (points // LEAF) + 7,)),

time: 24.9 us -> 24.9 us (level)
  no operation moved by 1% of the time
where the time goes in v6:
time: 24.9 us; the launch traced here: 24.8 us
  Pallas kernels  24.8 us (100%)
    pallas_call x1, Pallas kernels, exchange(): pl.pallas_call(functools.partial(exchange_kernel, inner, outer), out_shap...  23.5 us
    pallas_call x1, Pallas kernels, expand(): pl.pallas_call(expand_kernel, out_shape=jax.ShapeDtypeStruct((PROBES, poi...  1.24 us

profile of v6, /device:TPU:1, one launch (start us, length us, event | category | flops | bytes accessed | tf_op | source)
XLA Modules:
  0.0 24.8 jit_solution(8015815773196627389)
XLA Ops:
  0.0 23.5 %shard_map.55 = (f32[64,4096]{1,0:T(8,128)S(1)}, f32[64,256]{1,0:T(8,128)S(1)}, bf16[8,32,4096]{2,1,0:T(8,128)(2,1)S(1)}) custom-call(f32[3,4096]{1,0:T(4,128)} %coords_hbm.1, f32[1,4096]{1,0:T(1,128)} %bitcast.1, s32[1,4096]{1,0:T(1,128)} %order_hbm.1, bf16[64,4096]{1,0:T(8,128)(2,1)} %probes_hbm.1, bf16[10,2,32,4096]{3,2,1,0:T(8,128)(2,1)} %factors_hbm.1), custom_call_target="tpu_custom_call" | custom-call | tf_op jit(solution)/shard_map/pallas_call | solution.py:543
  23.5 1.2 %shard_map.56 = f32[64,4096]{1,0:T(8,128)} custom-call(f32[64,4096]{1,0:T(8,128)S(1)} %get-tuple-element.8.dense, f32[64,256]{1,0:T(8,128)S(1)} %get-tuple-element.9.sib, bf16[8,32,4096]{2,1,0:T(8,128)(2,1)S(1)} %get-tuple-element.10.left), custom_call_target="tpu_custom_call" | custom-call | tf_op jit(solution)/shard_map/pallas_call | solution.py:618
